TPU v7x, 256 devices: a whole 4x4x8 slice. The times are simulated.
256 devices in a mesh: dom: 32 (over y, x, core), head: 8 (over z).
Axes of the slice: x: 4, y: 4, z: 8, core: 2. Of those that a mesh axis runs over, the one named last changes fastest.
Arguments:
- features: bfloat16 [32768, 1024], P(('dom', 'head')), may hold values from -6 to 6
- norm_gain: float32 [1024], replicated, may hold values from 0.1 to 1.9
- in_proj: bfloat16 [1024, 3072], replicated, may hold values from -2.5 to 2.5, as said below
- out_proj: bfloat16 [1024, 1024], replicated, may hold values from -0.375 to 0.375
- adjacency: int32 [256, 8], P('dom'), may hold values from 0 to 255, as said below
- counts: int32 [256], P('dom'), may hold values from 3 to 8, as said below
Outputs:
- updated: bfloat16 [32768, 1024], P(('dom', 'head'))
Inputs may be any that keep to these rules, and one draw needn't show every extreme that they name: `in_proj`: columns h * 3 * 64 + c * 64 + e hold head h's query (c = 0), key (c = 1) and value (c = 2) component e. `adjacency`: row t holds 8 distinct tile numbers; entry 0 is t itself. With a partition being 8 consecutive tiles, every entry lies in t's partition or one of the two beside it; entry 1 lies in the partition before t's and entry 2 in the one after (in the first and last partition both lie in the only neighbouring one). Only the first counts[t] entries of row t of adjacency are used.
All inputs are finite; a program needn't handle non-finite values.
Results may differ from a plain program's by a relative error of at most 0.015.
The roundings to bfloat16 on the way count: a program that leaves them out, or rounds other values in their place, can miss the bound.
Values may be sent and summed in bfloat16 or wider, within the bound.
No kernel may reach another device: no remote copies, remote signals or barrier semaphores. Data moves between devices by JAX's collectives and lax.ppermute only.
A program may use at most 128 MiB of HBM per device.

v0:
```python
import math

import jax
import jax.numpy as jnp
from jax import lax
from jax.sharding import PartitionSpec as P

HEADS = 16
HEAD_DIM = 64
TILE = 128
NB = 8


epsilon = 1e-05


def padded(array, sides, width):
    for axis, dim in sides:
        size, length = (lax.axis_size(axis), array.shape[dim])
        up = [(i, (i + 1) % size) for i in range(size - 1)]
        down = [(j, i) for i, j in up]
        last = lax.slice_in_dim(array, length - width, length, axis=dim)
        first = lax.slice_in_dim(array, 0, width, axis=dim)
        before = lax.ppermute(last, axis, up)
        after = lax.ppermute(first, axis, down)
        array = jnp.concatenate([before, array, after], axis=dim)
    return array


def rms_normed(features, norm_gain):
    widened = features.astype(jnp.float32)
    power = jnp.mean(widened * widened, axis=-1, keepdims=True)
    return (widened, (widened * lax.rsqrt(power + epsilon) * norm_gain).astype(jnp.bfloat16))


def attend(queries, window, tile_lists, counts, head_share):
    query_rows = queries.shape[0]
    query_tiles = query_rows // TILE
    window_grid = window.reshape(window.shape[0] // TILE, TILE, head_share, 2, HEAD_DIM)
    block_tiles = math.gcd(query_tiles, max(1, 8 // head_share))
    blocks = query_tiles // block_tiles
    slot_tile = jnp.arange(NB * TILE) // TILE

    def one_block(pieces):
        query_block, list_block, count_block = pieces
        picked = window_grid[list_block]
        keys = picked[:, :, :, :, 0].reshape(block_tiles, NB * TILE, head_share, HEAD_DIM)
        values = picked[:, :, :, :, 1].reshape(block_tiles, NB * TILE, head_share, HEAD_DIM)
        scores = jnp.einsum(
            "bqhd,bkhd->bhqk", query_block, keys, preferred_element_type=jnp.float32
        ) * HEAD_DIM ** (-0.5)
        usable = slot_tile[None, :] < count_block[:, None]
        scores = jnp.where(usable[:, None, None, :], scores, -1e30)
        row_max = jnp.max(scores, axis=-1, keepdims=True)
        powers = jnp.exp(scores - row_max)
        totals = jnp.sum(powers, axis=-1, keepdims=True)
        weights = (powers / totals).astype(jnp.bfloat16)
        mixed = jnp.einsum("bhqk,bkhd->bqhd", weights, values, preferred_element_type=jnp.float32)
        return mixed.astype(jnp.bfloat16).reshape(block_tiles, TILE, head_share * HEAD_DIM)

    query_grid = queries.reshape(blocks, block_tiles, TILE, head_share, HEAD_DIM)
    result = lax.map(
        one_block,
        (
            query_grid,
            tile_lists.reshape(blocks, block_tiles, NB),
            counts.reshape(blocks, block_tiles),
        ),
    )
    return result.reshape(query_rows, head_share * HEAD_DIM)


def body(features, norm_gain, in_proj, out_proj, adjacency, counts):
    widened, normed = rms_normed(features, norm_gain)
    stacked = jnp.dot(normed, in_proj, preferred_element_type=jnp.float32).astype(jnp.bfloat16)
    local_rows = features.shape[0]
    head_count = lax.axis_size("head")
    group_rows = local_rows * head_count
    group_tiles = group_rows // TILE
    first_tile = (lax.axis_index("dom") - 1) * group_tiles
    local_lists = adjacency - first_tile
    layout = stacked.reshape(local_rows, HEADS, 3, HEAD_DIM)
    key_value = layout[:, :, 1:].reshape(local_rows, HEADS * 2 * HEAD_DIM)
    group_values = lax.all_gather(key_value, "head", axis=0, tiled=True)
    window = padded(group_values, (("dom", 0),), group_rows)
    own_tiles = local_rows // TILE
    start = lax.axis_index("head") * own_tiles
    own_lists = lax.dynamic_slice_in_dim(local_lists, start, own_tiles, 0)
    own_counts = lax.dynamic_slice_in_dim(counts, start, own_tiles, 0)
    by_node = attend(layout[:, :, 0], window, own_lists, own_counts, HEADS)
    return (widened + jnp.dot(by_node, out_proj, preferred_element_type=jnp.float32)).astype(
        jnp.bfloat16
    )


def solution(mesh):
    return jax.shard_map(
        body,
        mesh=mesh,
        in_specs=(P(("dom", "head"), None), P(), P(), P(), P("dom", None), P("dom")),
        out_specs=P(("dom", "head"), None),
        check_vma=False,
    )
```

profile of v0, /device:TPU:120, one launch (start us, length us, event | category | flops | bytes accessed | tf_op | source)
XLA Modules:
  0.0 197.6 jit_solution(10695451366262926060)
XLA Ops:
  6.5 0.0 copy-start
  6.5 0.0 all-gather.2.cloned.1.call-start
  6.5 1.2 fusion.10
  7.8 0.0 copy-start.3
  7.8 0.0 copy-start.2
  7.8 4.0 %convolution_convert_fusion = bf16[128,3072]{1,0:T(8,128)(2,1)S(1)} fusion(bf16[1024,3072]{1,0:T(8,128)(2,1)} %param.8, bf16[128,1024]{1,0:T(8,128)(2,1)} %param.6, f32[1024]{0:T(1024)} %param.7, f32[128]{0:T(128)S(1)} %add_rsqrt_fusion), kind=kOutput, calls=%fused_computation.11 | convolution fusion | flops 806223872 | bytes 7344640 | tf_op jit(solution)/shard_map/dot_general | solution.py:75
  11.8 1.2 copy.8
  13.0 1.9 slice.20
  14.8 0.0 all-gather.2.cloned.1.call-update
  14.9 62.7 %all-gather.2.cloned.1.call-done = bf16[1024,2048]{0,1:T(8,128)(2,1)} async-done(((bf16[128,2048]{0,1:T(8,128)(2,1)}), bf16[1024,2048]{0,1:T(8,128)(2,1)}) %all-gather.2.cloned.1.call-update) | async-done | bytes 4194320 | tf_op jit(solution)/shard_map/all_gather | solution.py:84
  77.6 1.9 collective-permute-start.1
  79.5 2.4 %collective-permute-start = (bf16[1024,2048]{0,1:T(8,128)(2,1)}, bf16[1024,2048]{0,1:T(8,128)(2,1)}, u32[]{:S(2)}, u32[]{:S(2)}) collective-permute-start(bf16[1024,2048]{0,1:T(8,128)(2,1)} %all-gather.2.cloned.1.call-done), channel_id=1, source_target_pairs={{0,8},{8,16},{16,24},{24,32},{32,40},{40,48},{48,56},{56,64},{64,7... | collective-permute-start | bytes 12582920 | tf_op jit(solution)/shard_map/ppermute | solution.py:24
  81.9 0.0 copy-done.3
  81.9 0.6 dynamic_slice.16
  82.5 0.0 copy-done.2
  82.5 0.7 fusion.17
  83.2 42.6 %collective-permute-done.1 = bf16[1024,2048]{0,1:T(8,128)(2,1)} collective-permute-done((bf16[1024,2048]{0,1:T(8,128)(2,1)}, bf16[1024,2048]{0,1:T(8,128)(2,1)}, u32[]{:S(2)}, u32[]{:S(2)}) %collective-permute-start.1) | collective-permute-done | bytes 4194336 | tf_op jit(solution)/shard_map/ppermute | solution.py:25
  125.8 5.9 %collective-permute-done = bf16[1024,2048]{0,1:T(8,128)(2,1)} collective-permute-done((bf16[1024,2048]{0,1:T(8,128)(2,1)}, bf16[1024,2048]{0,1:T(8,128)(2,1)}, u32[]{:S(2)}, u32[]{:S(2)}) %collective-permute-start) | collective-permute-done | bytes 4194336 | tf_op jit(solution)/shard_map/ppermute | solution.py:24
  131.7 6.0 %maximum_bitcast_fusion = bf16[256,8,24,128]{3,1,2,0:T(8,128)(2,1)S(1)} fusion(bf16[1024,2048]{0,1:T(8,128)(2,1)} %collective-permute-done.1, bf16[1024,2048]{0,1:T(8,128)(2,1)} %all-gather.2.cloned.1.call-done, bf16[1024,2048]{0,1:T(8,128)(2,1)} %collective-permute-done), kind=kLoop, calls=%fused_computation.2 | loop fusion | flops 37748736 | bytes 25165824
  137.8 3.2 %copy.14 = bf16[256,8,24,128]{3,2,1,0:T(8,128)(2,1)S(1)} copy(bf16[256,8,24,128]{3,1,2,0:T(8,128)(2,1)S(1)} %maximum_bitcast_fusion) | data formatting | bytes 25165824
  140.9 6.7 %copy.9 = bf16[24,128,16,2,64]{1,4,3,2,0:T(8,128)(2,1)} copy(bf16[24,128,16,2,64]{1,0,4,3,2:T(8,128)(2,1)S(1)} %bitcast.45) | data formatting | bytes 25165824 | tf_op jit(solution)/shard_map/reshape | solution.py:39
  147.6 7.6 %gather_fusion = bf16[8,128,16,2,64]{1,4,3,2,0:T(8,128)(2,1)} fusion(bf16[24,128,16,2,64]{1,4,3,2,0:T(8,128)(2,1)} %copy.9, s32[1024]{0:T(1024)S(1)} %pad_clamp_fusion), kind=kCustom, calls=%fused_computation | custom fusion | bytes 8388640 | tf_op jit(solution)/shard_map/while/body/eval_jaxpr/gather | solution.py:46
  155.2 4.5 %fusion.24 = (bf16[1,8,128,16,1,64]{2,5,4,3,1,0:T(8,128)(2,1)}, bf16[1,8,128,16,1,64]{2,5,4,3,1,0:T(8,128)(2,1)S(1)}) fusion(bf16[1,8,128,16,2,64]{2,5,4,3,1,0:T(8,128)(2,1)} %bitcast.46), kind=kLoop, calls=%fused_computation.40 | loop fusion | bytes 8388608 | tf_op jit(solution)/shard_map/while/body/eval_jaxpr/slice | solution.py:47
  159.7 3.1 %copy.10 = bf16[1,8,128,16,1,64]{2,1,5,3,4,0:T(8,128)(2,1)} copy(bf16[1,8,128,16,1,64]{2,5,4,3,1,0:T(8,128)(2,1)S(1)} %get-tuple-element.18) | data formatting | bytes 4194304 | tf_op jit(solution)/shard_map/while/body/eval_jaxpr/slice | solution.py:48
  162.9 4.2 %reshape.88 = bf16[1024,16,64]{0,2,1:T(8,128)(2,1)} reshape(bf16[1,8,128,16,1,64]{2,1,5,3,4,0:T(8,128)(2,1)} %copy.10) | data formatting | bytes 4194304 | tf_op jit(solution)/shard_map/reshape.19
  167.1 4.7 %copy.12 = bf16[1,8,128,16,1,64]{2,1,5,3,4,0:T(8,128)(2,1)} copy(bf16[1,8,128,16,1,64]{2,5,4,3,1,0:T(8,128)(2,1)} %get-tuple-element.17) | data formatting | bytes 4194304 | tf_op jit(solution)/shard_map/while/body/eval_jaxpr/slice | solution.py:47
  171.7 4.2 %reshape.90 = bf16[1024,16,64]{0,2,1:T(8,128)(2,1)} reshape(bf16[1,8,128,16,1,64]{2,1,5,3,4,0:T(8,128)(2,1)} %copy.12) | data formatting | bytes 4194304 | tf_op jit(solution)/shard_map/reshape.15
  175.9 7.9 %fusion.25 = (f32[16,128]{1,0:T(8,128)S(1)}, f32[16,128,1024]{2,1,0:T(8,128)}) fusion(pred[1024]{0:T(1024)(128)(4,1)S(1)} %fusion.17, bf16[1024,16,64]{0,2,1:T(8,128)(2,1)} %reshape.90, bf16[128,16,3,64]{0,3,2,1:T(8,128)(2,1)} %bitcast.48), kind=kOutput, calls=%fused_computation.41 | convolution fusion | flops 276825088 | bytes 10757120 | tf_op jit(solution)/shard_map/while/body/eval_jaxpr/sub | solution.py:55
  183.8 5.7 %fusion.6 = bf16[16,64,128]{2,1,0:T(8,128)(2,1)S(1)} fusion(bf16[1024,16,64]{0,2,1:T(8,128)(2,1)} %reshape.88, f32[16,128,1024]{2,1,0:T(8,128)} %get-tuple-element.20, f32[16,128]{1,0:T(8,128)S(1)} %get-tuple-element.19), kind=kOutput, calls=%fused_computation.13 | convolution fusion | flops 272760832 | bytes 10756096 | tf_op jit(solution)/shard_map/while/body/eval_jaxpr/bhqk,bkhd->bqhd/dot_general | solution.py:58
  189.5 0.0 copy-done
  189.5 0.0 copy-done.1
  189.5 1.2 fusion.7
  (5 shorter events, 0.0 us)
Async XLA Ops:
  6.5 183.0 %copy-start = (bf16[1024,1024]{1,0:T(8,128)(2,1)S(1)}, bf16[1024,1024]{1,0:T(8,128)(2,1)}, u32[]{:S(2)}) copy-start(bf16[1024,1024]{1,0:T(8,128)(2,1)} %param.9) | copy-start | bytes 6291460
  6.5 71.0 %all-gather.2.cloned.1.call-start = ((), (), s32[]{:S(2)}) async-start(), calls=%async_computation | async-start | bytes 4718592 | tf_op jit(solution)/shard_map/all_gather | solution.py:84
  7.8 74.1 %copy-start.3 = (s32[8]{0:T(128)S(1)}, s32[8]{0:T(128)}, u32[]{:S(2)}) copy-start(s32[8]{0:T(128)} %param.11) | copy-start | bytes 100
  7.8 74.7 %copy-start.2 = (s32[8,8]{1,0:T(8,128)S(1)}, s32[8,8]{1,0:T(8,128)}, u32[]{:S(2)}) copy-start(s32[8,8]{1,0:T(8,128)} %param.10) | copy-start | bytes 772
  77.6 48.2 %collective-permute-start.1 = (bf16[1024,2048]{0,1:T(8,128)(2,1)}, bf16[1024,2048]{0,1:T(8,128)(2,1)}, u32[]{:S(2)}, u32[]{:S(2)}) collective-permute-start(bf16[1024,2048]{0,1:T(8,128)(2,1)} %all-gather.2.cloned.1.call-done), channel_id=1, source_target_pairs={{8,0},{16,8},{24,16},{32,24},{40,32},{48,40},{56,48},{64,56},{72,6... | collective-permute-start | bytes 12582920 | tf_op jit(solution)/shard_map/ppermute | solution.py:25
  79.5 52.2 %collective-permute-start = (bf16[1024,2048]{0,1:T(8,128)(2,1)}, bf16[1024,2048]{0,1:T(8,128)(2,1)}, u32[]{:S(2)}, u32[]{:S(2)}) collective-permute-start(bf16[1024,2048]{0,1:T(8,128)(2,1)} %all-gather.2.cloned.1.call-done), channel_id=1, source_target_pairs={{0,8},{8,16},{16,24},{24,32},{32,40},{40,48},{48,56},{56,64},{64,7... | collective-permute-start | bytes 12582920 | tf_op jit(solution)/shard_map/ppermute | solution.py:24
  183.8 5.7 %copy-start.1 = (bf16[128,1024]{1,0:T(8,128)(2,1)S(1)}, bf16[128,1024]{1,0:T(8,128)(2,1)}, u32[]{:S(2)}) copy-start(bf16[128,1024]{1,0:T(8,128)(2,1)} %param.6) | copy-start | bytes 786436
Sparse Core Ops, SparseCore 0:
  15.0 62.5 all-gather.1
where the time goes:
time: 201 us; the launch traced here: 198 us
  waiting for transfers between devices  111 us (55%)
  local copies, waits for them, and re-layouts  41.8 us (21%)
  matrix products  18.7 us (9%)
  between operations  13.5 us (7%)
  other arithmetic  7.93 us (4%)
  starting transfers between devices  4.32 us (2%)
    all_gather x1, waiting for transfers between devices, body(): group_values = lax.all_gather(key_value, 'head', axis=0, tiled=True)  62.7 us
    ppermute x1, waiting for transfers between devices, padded(): after = lax.ppermute(first, axis, down)  42.6 us
    slice x2, local copies, waits for them, and re-layouts, one_block(): picked[:, :, :, :, 0].reshape(block_tiles, NB * TILE, head_share, HEAD_DIM)  9.2 us
    another operation x2, local copies, waits for them, and re-layouts  8.36 us
    sub x1, matrix products, one_block(): powers = jnp.exp(scores - row_max)  7.88 us
    gather x1, local copies, waits for them, and re-layouts, one_block(): picked = window_grid[list_block]  7.6 us
    reshape x1, local copies, waits for them, and re-layouts, attend(): window.reshape(window.shape[0] // TILE, TILE, head_share, 2, HEAD_DIM)  6.67 us
    unnamed x1, other arithmetic  6.02 us
  transfers between devices with their start and end apart: 3, of which 3 were waited for; matrix products, arithmetic and copies ran while one was open for 1% of the time, Pallas kernels for 0%

commit v1 on v0

v1 whole, which is shorter than its diff:
```python
import functools

import jax
import jax.numpy as jnp
from jax import lax
from jax.experimental import pallas as pl
from jax.experimental.pallas import tpu as pltpu
from jax.sharding import PartitionSpec as P

HEADS = 16
HEAD_DIM = 64
TILE = 128
NB = 8
D = 1024
PAIRS = HEADS // 2
STATS = 4 * HEADS
PARTS = 8
LOW = -1e30
epsilon = 1e-05
VMEM = pl.BlockSpec(memory_space=pltpu.VMEM)
SMEM = pl.BlockSpec(memory_space=pltpu.SMEM)
PARAMS = pltpu.CompilerParams(vmem_limit_bytes=40 * 1024 * 1024)


def normed(features, gain):
    wide = features.astype(jnp.float32)
    power = jnp.mean(wide * wide, axis=-1, keepdims=True)
    return (wide * lax.rsqrt(power + epsilon) * gain).astype(jnp.bfloat16)


def prepare_kernel(
    features_ref, adjacency_ref, counts_ref, w_ref, parcel_ref, q_ref, kv_ref, lists_ref, amounts_ref, held_ref, sems
):
    rows = D // PARTS
    copies = [
        pltpu.make_async_copy(features_ref, parcel_ref.at[pl.ds(0, TILE)], sems.at[0]),
        pltpu.make_async_copy(adjacency_ref, lists_ref, sems.at[1]),
        pltpu.make_async_copy(counts_ref, amounts_ref, sems.at[2]),
    ]
    for i in range(PARTS):
        at = pl.ds(i * rows, rows)
        copies.append(pltpu.make_async_copy(w_ref.at[at], held_ref.at[at], sems.at[3 + i]))
    for copy in copies:
        copy.start()
    for copy in copies[:3]:
        copy.wait()
    lists = jnp.concatenate([lists_ref[...], amounts_ref[...], jnp.zeros((7, NB), jnp.int32)], axis=0)
    parcel_ref[pl.ds(TILE, 16)] = jnp.zeros((16, D), jnp.bfloat16)
    parcel_ref[pl.ds(TILE, 16), :NB] = lists.astype(jnp.float32).astype(jnp.bfloat16)
    low = lax.broadcasted_iota(jnp.int32, (rows, 128), 1) < HEAD_DIM
    for i, copy in enumerate(copies[3:]):
        copy.wait()
        at = pl.ds(i * rows, rows)
        for j in range(PAIRS):
            t0, t1, t2 = (held_ref[at, pl.ds(j * 384 + c * 128, 128)] for c in range(3))
            q_ref[at, pl.ds(j * 128, 128)] = jnp.where(low, t0, t1)
            kv_ref[at, pl.ds(j * 128, 128)] = jnp.where(low, t2, t0)
            kv_ref[at, pl.ds(D + j * 128, 128)] = jnp.where(low, t1, t2)


def prepare(features, adjacency, counts, in_proj):
    arrays = (features, adjacency, counts, in_proj)
    return pl.pallas_call(
        prepare_kernel,
        in_specs=[pl.BlockSpec(memory_space=pltpu.HBM)] * 4,
        out_specs=[VMEM] * 3,
        out_shape=[
            jax.ShapeDtypeStruct((TILE + 16, D), jnp.bfloat16),
            jax.ShapeDtypeStruct((D, D), jnp.bfloat16),
            jax.ShapeDtypeStruct((D, 2 * D), jnp.bfloat16),
        ],
        scratch_shapes=[
            pltpu.VMEM((NB, NB), jnp.int32),
            pltpu.VMEM((1, NB), jnp.int32),
            pltpu.VMEM((D, 3 * D), jnp.bfloat16),
            pltpu.SemaphoreType.DMA((3 + PARTS,)),
        ],
        compiler_params=PARAMS,
        cost_estimate=pl.CostEstimate(flops=0, bytes_accessed=12 * 1024 * 1024, transcendentals=0),
        name="prepare",
    )(*(pltpu.with_memory_space_constraint(a, pltpu.HBM) for a in arrays))


def project_queries(rows, w_ref, q_ref, n):
    for c in range(2):
        part = jnp.dot(rows, w_ref[:, c * 512 : (c + 1) * 512], preferred_element_type=jnp.float32)
        part = part.astype(jnp.bfloat16).astype(jnp.float32) * HEAD_DIM ** (-0.5)
        for j in range(4):
            turned = pltpu.roll(part[:, j * 128 : (j + 1) * 128], HEAD_DIM, 1)
            q_ref[n, :, c * 512 + j * 128 : c * 512 + (j + 1) * 128] = turned.astype(jnp.bfloat16)


def near_kernel(core_ref, cross_ref, parcel_ref, gain_ref, w_ref, q_ref, info_ref):
    here, group = lax.axis_index("head"), lax.axis_index("dom")
    row = lax.broadcasted_iota(jnp.int32, (16, 128), 0)
    lane = lax.broadcasted_iota(jnp.int32, (16, 128), 1)
    info = jnp.zeros((1, 1), jnp.float32)
    for n, ref in enumerate((parcel_ref, core_ref, cross_ref)):
        if n > 0:
            project_queries(normed(ref[:TILE], gain_ref[...]), w_ref, q_ref, n - 1)
        lists = ref[pl.ds(TILE, 16), :128].astype(jnp.float32).astype(jnp.int32)
        count = jnp.where((row == NB) & (lane == here), lists, 0).astype(jnp.float32)
        count = jnp.sum(jnp.sum(count, axis=0, keepdims=True), axis=1, keepdims=True)
        used = (row == here) & (lane < jnp.minimum(count, NB).astype(jnp.int32))
        used = used & (jnp.right_shift(lists, 3) == group)
        bits = jnp.where(used, jnp.left_shift(1, (lists & (NB - 1)) + n * NB), 0).astype(jnp.float32)
        info = info + jnp.sum(jnp.sum(bits, axis=0, keepdims=True), axis=1, keepdims=True)
    info_ref[...] = jnp.broadcast_to(info, info_ref.shape)


def project_near(core, cross, parcel, gain, w_query):
    return pl.pallas_call(
        near_kernel,
        in_specs=[VMEM] * 5,
        out_specs=[VMEM] * 2,
        out_shape=[
            jax.ShapeDtypeStruct((2, TILE, D), jnp.bfloat16),
            jax.ShapeDtypeStruct((8, 128), jnp.float32),
        ],
        compiler_params=PARAMS,
        cost_estimate=pl.CostEstimate(
            flops=4 * TILE * D * D, bytes_accessed=4 * 1024 * 1024, transcendentals=0
        ),
        name="project_near",
    )(core, cross, parcel, gain, w_query)


def project_kernel(count, with_query, *refs):
    features, gain_ref, refs = refs[:count], refs[count], refs[count + 1 :]
    if with_query:
        wq_ref, w_ref, q_ref, k_ref, vt_ref, rows_ref = refs
    else:
        w_ref, k_ref, vt_ref, rows_ref = refs
    at = 0
    for ref in features:
        rows_ref[at : at + ref.shape[0]] = normed(ref[...], gain_ref[...])
        at += ref.shape[0]
    if with_query:
        project_queries(rows_ref[:TILE], wq_ref, q_ref, 0)
    for c in range(2):
        at = slice(c * 512, (c + 1) * 512)
        part = jnp.dot(rows_ref[...], w_ref[:, at], preferred_element_type=jnp.float32)
        k_ref[:, at] = part.astype(jnp.bfloat16)
    for c in range(2):
        at, cols = slice(c * 512, (c + 1) * 512), slice(D + c * 512, D + (c + 1) * 512)
        part = jnp.dot(rows_ref[...], w_ref[:, cols], preferred_element_type=jnp.float32)
        vt_ref[at] = part.T.astype(jnp.bfloat16)


def project(arrays, gain, w_kv, w_query=None):
    total, query = sum(a.shape[0] for a in arrays), w_query is not None
    return pl.pallas_call(
        functools.partial(project_kernel, len(arrays), query),
        in_specs=[VMEM] * (len(arrays) + 2 + query),
        out_specs=[VMEM] * (2 + query),
        out_shape=[jax.ShapeDtypeStruct((1, TILE, D), jnp.bfloat16)] * query
        + [
            jax.ShapeDtypeStruct((total, D), jnp.bfloat16),
            jax.ShapeDtypeStruct((D, total), jnp.bfloat16),
        ],
        scratch_shapes=[pltpu.VMEM((total, D), jnp.bfloat16)],
        compiler_params=PARAMS,
        cost_estimate=pl.CostEstimate(
            flops=4 * total * D * D, bytes_accessed=5 * 1024 * 1024, transcendentals=0
        ),
        name="project",
    )(*arrays, gain, *([w_query] * query), w_kv)


def attend_tile(q_ref, k_ref, vt_ref, at, m_ref, l_ref, acc_ref):
    low = lax.broadcasted_iota(jnp.int32, (TILE, 128), 1) < HEAD_DIM
    old, total = m_ref[...], l_ref[...]
    scores, powers, tops, sums = [], [], [], []
    for j in range(PAIRS):
        cols = slice(j * 128, (j + 1) * 128)
        query = q_ref[:, cols]
        zero = jnp.zeros_like(query)
        both = jnp.concatenate([jnp.where(low, query, zero), jnp.where(low, zero, query)], axis=0)
        scores.append(
            lax.dot_general(
                k_ref[at : at + TILE, cols],
                both,
                (((1,), (1,)), ((), ())),
                preferred_element_type=jnp.float32,
            )
        )
    for j in range(PAIRS):
        top = jnp.maximum(old[j : j + 1], jnp.max(scores[j], axis=0, keepdims=True))
        power = jnp.exp(scores[j] - top)
        tops.append(top)
        sums.append(jnp.sum(power, axis=0, keepdims=True))
        powers.append(power.astype(jnp.bfloat16))
    new = jnp.concatenate(tops, axis=0)
    fade = jnp.exp(old - new)
    m_ref[...] = new
    l_ref[...] = total * fade + jnp.concatenate(sums, axis=0)
    for j in range(PAIRS):
        for half, lanes in ((0, slice(TILE, 2 * TILE)), (1, slice(0, TILE))):
            rows = slice(j * 128 + half * HEAD_DIM, j * 128 + (half + 1) * HEAD_DIM)
            mixed = jnp.dot(
                vt_ref[rows, at : at + TILE], powers[j][:, lanes], preferred_element_type=jnp.float32
            )
            acc_ref[rows] = acc_ref[rows] * fade[j : j + 1, lanes] + mixed


def attend_kernel(who, steps, first, last, *refs):
    info_ref, q_refs, refs = refs[0], refs[1 : 1 + len(who)], refs[1 + len(who) :]
    keys, refs = refs[: 2 * len(steps)], refs[2 * len(steps) :]
    if not first:
        refs = refs[3:]
    m_ref, l_ref, acc_ref = refs[:3]
    if first:
        m_ref[...] = jnp.full_like(m_ref, LOW)
        l_ref[...] = jnp.zeros_like(l_ref)
        acc_ref[...] = jnp.zeros_like(acc_ref)
    here, turn = lax.axis_index("head"), 1 - 2 * (lax.axis_index("dom") % 2)
    info = jnp.max(info_ref[...]).astype(jnp.int32)
    for n, (q_ref, (flag, row)) in enumerate(zip(q_refs, who)):
        for s, shifts in enumerate(steps):
            k_ref, vt_ref = keys[2 * s], keys[2 * s + 1]
            for place, shift in enumerate(shifts):
                tile = lax.rem(here + turn * shift + 8, 8)

                @pl.when(jnp.right_shift(info, flag * NB + tile) & 1 != 0)
                def _():
                    attend_tile(
                        q_ref.at[row], k_ref, vt_ref, place * TILE, m_ref.at[n], l_ref.at[n], acc_ref.at[n]
                    )

    if not last:
        return
    n, out_ref = len(who) - 1, refs[3]
    total = l_ref[n]
    some = total > 0
    safe = jnp.where(some, total, 1.0)
    inverse = 1.0 / safe
    lse = jnp.where(some, m_ref[n] + jnp.log(safe), LOW)
    for j in range(PAIRS):
        even, odd = pl.ds(j * 128, HEAD_DIM), pl.ds(j * 128 + HEAD_DIM, HEAD_DIM)
        out_ref[even] = (acc_ref[n, even] * inverse[j : j + 1, TILE:]).astype(jnp.bfloat16)
        out_ref[odd] = (acc_ref[n, odd] * inverse[j : j + 1, :TILE]).astype(jnp.bfloat16)
    stacked = jnp.concatenate([lse[:, :TILE], lse[:, TILE:]], axis=0)
    for c in range(3):
        term = stacked.astype(jnp.bfloat16)
        out_ref[pl.ds(D + c * HEADS, HEADS)] = term
        stacked = stacked - term.astype(jnp.float32)
    out_ref[pl.ds(D + 3 * HEADS, HEADS)] = jnp.ones((HEADS, TILE), jnp.bfloat16)


def attend(info, queries, kv, state=(), last=False):
    who, steps = [q[1:] for q in queries], [shifts for shifts, _, _ in kv]
    arrays = [q[0] for q in queries] + [a for _, k, vt in kv for a in (k, vt)]
    at = 1 + len(arrays)
    return pl.pallas_call(
        functools.partial(attend_kernel, who, steps, not state, last),
        in_specs=[VMEM] * (at + len(state)),
        out_specs=[VMEM] * (4 if last else 3),
        out_shape=[
            jax.ShapeDtypeStruct((len(who), PAIRS, 2 * TILE), jnp.float32),
            jax.ShapeDtypeStruct((len(who), PAIRS, 2 * TILE), jnp.float32),
            jax.ShapeDtypeStruct((len(who), D, TILE), jnp.float32),
        ]
        + [jax.ShapeDtypeStruct((D + STATS, TILE), jnp.bfloat16)] * last,
        input_output_aliases={at + i: i for i in range(len(state))},
        compiler_params=PARAMS,
        cost_estimate=pl.CostEstimate(
            flops=16 * TILE * TILE * D * len(kv), bytes_accessed=4 * 1024 * 1024, transcendentals=0
        ),
        name="attend",
    )(info, *arrays, *state)


def split(x):
    return jnp.concatenate([x[:, :TILE], x[:, TILE:]], axis=0)


def received(ref):
    terms = [ref[pl.ds(D + c * HEADS, HEADS)].astype(jnp.float32) for c in range(4)]
    return jnp.where(terms[3] > 0, terms[0] + terms[1] + terms[2], LOW)


def first_kernel(m_ref, l_ref, cross_ref, lse_ref):
    lse_ref[0] = split(m_ref[0]) + jnp.log(split(l_ref[0]))
    lse_ref[1] = received(cross_ref)


def finish_first(m, l, cross):
    return pl.pallas_call(
        first_kernel,
        in_specs=[VMEM] * 3,
        out_specs=VMEM,
        out_shape=jax.ShapeDtypeStruct((2, HEADS, TILE), jnp.float32),
        compiler_params=PARAMS,
        cost_estimate=pl.CostEstimate(flops=0, bytes_accessed=2 * 1024 * 1024, transcendentals=0),
        name="finish_first",
    )(m, l, cross)


def finish_kernel(lse_ref, l_ref, own_ref, core_ref, cross_ref, w_ref, features_ref, out_ref, sum_ref, made_ref, sems):
    total = split(l_ref[0])
    lse = [lse_ref[0], received(core_ref), lse_ref[1]]
    top = jnp.maximum(jnp.maximum(lse[0], lse[1]), lse[2])
    parts = [jnp.exp(x - top) for x in lse]
    inverse = 1.0 / (parts[0] + parts[1] + parts[2])
    scale = [parts[0] * inverse / total, parts[1] * inverse, parts[2] * inverse]
    for h in range(HEADS):
        row = h // 2 + (PAIRS if h % 2 == 0 else 0)
        at = pl.ds(h * HEAD_DIM, HEAD_DIM)
        mixed = own_ref[0, at] * scale[0][row : row + 1]
        mixed += core_ref[at].astype(jnp.float32) * scale[1][row : row + 1]
        mixed += cross_ref[at].astype(jnp.float32) * scale[2][row : row + 1]
        sum_ref[at] = mixed
    attended = sum_ref[...].T.astype(jnp.bfloat16)
    copies = []
    for c in range(4):
        at = pl.ds(c * 256, 256)
        product = jnp.dot(attended, w_ref[:, at], preferred_element_type=jnp.float32)
        made_ref[:, at] = (features_ref[:, at].astype(jnp.float32) + product).astype(jnp.bfloat16)
        copies.append(pltpu.make_async_copy(made_ref.at[:, at], out_ref.at[:, at], sems.at[c]))
        copies[-1].start()
    for copy in copies:
        copy.wait()


def finish(state, core, cross, out_proj, features):
    m, l, own = state
    lse = finish_first(m, l, cross)
    return pl.pallas_call(
        finish_kernel,
        in_specs=[VMEM] * 7,
        out_specs=pl.BlockSpec(memory_space=pl.ANY),
        out_shape=jax.ShapeDtypeStruct((TILE, D), jnp.bfloat16),
        scratch_shapes=[
            pltpu.VMEM((D, TILE), jnp.float32),
            pltpu.VMEM((TILE, D), jnp.bfloat16),
            pltpu.SemaphoreType.DMA((4,)),
        ],
        compiler_params=PARAMS,
        cost_estimate=pl.CostEstimate(
            flops=2 * TILE * D * D, bytes_accessed=4 * 1024 * 1024, transcendentals=0
        ),
        name="finish",
    )(lse, l, own, core, cross, out_proj, features)


def body(features, norm_gain, in_proj, out_proj, adjacency, counts):
    here, group = lax.axis_index("head"), lax.axis_index("dom")
    group_count, around = lax.axis_size("dom"), lax.axis_size("head")
    gain = norm_gain.reshape(1, D)

    up = [
        (p * around + i, p * around + (i + (-1) ** p) % around)
        for p in range(group_count)
        for i in range(around)
    ]
    up, down = (("dom", "head"), up), (("dom", "head"), [(j, i) for i, j in up])
    swap = [(i, i ^ 1) for i in range(group_count)]
    hop = [(i, i + 1) for i in range(1, group_count - 1, 2)]
    hop = hop + [(j, i) for i, j in hop]

    def tied(x, *others):
        return lax.optimization_barrier((x, *others))[0]

    one = [lax.ppermute(features, *up)]
    parcel, w_query, w_kv = prepare(features, adjacency, counts.reshape(1, NB), in_proj)
    two = [lax.ppermute(tied(features, parcel), *down)]
    from_cross = lax.ppermute(parcel, "dom", hop)
    from_core = lax.ppermute(parcel, "dom", swap)

    one.append(lax.ppermute(tied(one[0], w_query), *up))
    q_own, *kv_a = project([features, one[0]], gain, w_kv, w_query)
    two.append(lax.ppermute(tied(two[0], *kv_a), *down))
    q_near, info = project_near(from_core, from_cross, parcel, gain, w_query)
    kv_a = ((0, -1), *kv_a)
    pair, far = [(q_own, 0, 0), (q_near, 1, 0)], [(q_near, 2, 1)]

    one.append(lax.ppermute(tied(one[1], q_near), *up))
    kv_b = project([two[0], one[1]], gain, w_kv)
    two.append(lax.ppermute(tied(two[1], *kv_b), *down))
    kv_b = ((1, -2), *kv_b)
    far_state = attend(info, far, [kv_a, kv_b])

    one.append(lax.ppermute(tied(one[2], *far_state), *up))
    kv_c = ((2, -3), *project([two[1], one[2]], gain, w_kv))
    kv_d = ((3,), *project([two[2]], gain, w_kv))
    far_state = attend(info, far, [kv_c, kv_d], far_state)

    kv_e = ((4,), *project([tied(one[3], *far_state)], gain, w_kv))
    *_, to_cross = attend(info, far, [kv_e], far_state, last=True)
    cross = lax.ppermute(to_cross, "dom", hop)
    *pair_state, to_core = attend(
        tied(info, to_cross), pair, [kv_a, kv_b, kv_c, kv_d, kv_e], last=True
    )
    core = lax.ppermute(to_core, "dom", swap)
    return finish(pair_state, core, cross, out_proj, features)


def solution(mesh):
    return jax.shard_map(
        body,
        mesh=mesh,
        in_specs=(P(("dom", "head"), None), P(), P(), P(), P("dom", None), P("dom")),
        out_specs=P(("dom", "head"), None),
        check_vma=False,
    )
```

time: 201 us -> 50.7 us (0.25); the launches traced: 198 us -> 49.9 us
  waiting for transfers between devices: 111 us -> 13.4 us
  local copies, waits for them, and re-layouts: 41.8 us -> 0.01 us
  matrix products: 18.7 us -> 0 us
  starting transfers between devices: 4.32 us -> 20.9 us
  Pallas kernels: 0 us -> 15.2 us
  between operations: 13.5 us -> 0.34 us
  other arithmetic: 7.93 us -> 0 us
    all_gather x1 -> x0, waiting for transfers between devices: 62.7 us -> none  [body(): group_values = lax.all_gather(key_value, 'head', axis=0, tiled=True)]
    ppermute x2 -> x11, waiting for transfers between devices: 48.5 us -> 13.4 us  [the longest x1 4.14 us: body(): cross = lax.ppermute(to_cross, 'dom', hop)]
    ppermute x2 -> x11, starting transfers between devices: 4.32 us -> 20.9 us  [the longest x1 4.03 us: body(): from_cross = lax.ppermute(parcel, 'dom', hop)]
    pallas_call x0 -> x13, Pallas kernels: none -> 15.2 us  [the longest x5 6.4 us: project(): pl.pallas_call(functools.partial(project_kernel, len(arrays), query), in_...]
    slice x4 -> x0, local copies, waits for them, and re-layouts: 14.2 us -> none  [the longest x2 9.2 us: one_block(): picked[:, :, :, :, 0].reshape(block_tiles, NB * TILE, head_share, HEAD_DIM)]
    dot_general x3 -> x0, matrix products: 10.9 us -> none  [the longest x1 5.7 us: one_block(): jnp.einsum('bhqk,bkhd->bqhd', weights, values, preferred_element_type=jnp...]
    another operation x2 -> x0, local copies, waits for them, and re-layouts: 8.36 us -> none
    sub x1 -> x0, matrix products: 7.88 us -> none  [one_block(): powers = jnp.exp(scores - row_max)]
  transfers between devices with their start and end apart: 3 -> 11, of which waited for: 3 -> 6; matrix products, arithmetic and copies ran while one was open for 1% -> 0% of each run, Pallas kernels for 0% -> 26%
where the time goes in v1:
time: 50.7 us; the launch traced here: 49.9 us
  starting transfers between devices  20.9 us (41%)
  Pallas kernels  15.2 us (30%)
  waiting for transfers between devices  13.4 us (26%)
    pallas_call x5, Pallas kernels, project(): pl.pallas_call(functools.partial(project_kernel, len(arrays), query), in_...  6.4 us
    ppermute x1, waiting for transfers between devices, body(): cross = lax.ppermute(to_cross, 'dom', hop)  4.14 us
    ppermute x1, starting transfers between devices, body(): from_cross = lax.ppermute(parcel, 'dom', hop)  4.03 us
    ppermute x1, waiting for transfers between devices, body(): one.append(lax.ppermute(tied(one[1], q_near), *up))  3.98 us
    ppermute x1, starting transfers between devices, body(): one.append(lax.ppermute(tied(one[2], *far_state), *up))  3.69 us
    ppermute x1, starting transfers between devices, body(): one.append(lax.ppermute(tied(one[1], q_near), *up))  3.43 us
    pallas_call x4, Pallas kernels, attend(): pl.pallas_call(functools.partial(attend_kernel, who, steps, not state, la...  3.39 us
    pallas_call x1, Pallas kernels, prepare(): pl.pallas_call(prepare_kernel, in_specs=[pl.BlockSpec(memory_space=pltpu....  3.18 us
  transfers between devices with their start and end apart: 11, of which 6 were waited for; matrix products, arithmetic and copies ran while one was open for 0% of the time, Pallas kernels for 26%

profile of v1, /device:TPU:120, one launch (start us, length us, event | category | flops | bytes accessed | tf_op | source)
XLA Modules:
  0.0 49.9 jit_solution(8652941632022730277)
XLA Ops:
  0.0 3.1 %collective-permute-start.2 = (bf16[128,1024]{1,0:T(8,128)(2,1)}, bf16[128,1024]{1,0:T(8,128)(2,1)S(1)}, u32[]{:S(2)}, u32[]{:S(2)}) collective-permute-start(bf16[128,1024]{1,0:T(8,128)(2,1)} %features_ref.3), channel_id=1, source_target_pairs={{0,1},{1,2},{2,3},{3,4},{4,5},{5,6},{6,7},{7,0},{8,15},{9,8},{10,9... | collective-permute-start | bytes 786440 | tf_op jit(solution)/shard_map/ppermute | solution.py:364
  3.1 3.2 %prepare.1 = (bf16[144,1024]{1,0:T(8,128)(2,1)S(1)}, bf16[1024,1024]{1,0:T(8,128)(2,1)S(1)}, bf16[1024,2048]{1,0:T(8,128)(2,1)S(1)}) custom-call(bf16[128,1024]{1,0:T(8,128)(2,1)} %features_ref.3, s32[8,8]{1,0:T(8,128)} %adjacency_ref.1, s32[1,8]{1,0:T(1,128)} %bitcast.8, bf16[1024,3072]{1,0:T(8,128)(2,1)} %w_ref.2), custom_call_target="tpu_custom_call" | custom-call | bytes 12582912 | tf_op jit(solution)/shard_map/prepare/pallas_call | solution.py:63
  6.3 0.1 collective-permute-start.5
  6.4 4.0 %collective-permute-start.1 = (bf16[144,1024]{1,0:T(8,128)(2,1)S(1)}, bf16[144,1024]{1,0:T(8,128)(2,1)S(1)}, u32[]{:S(2)}, u32[]{:S(2)}) collective-permute-start(bf16[144,1024]{1,0:T(8,128)(2,1)S(1)} %get-tuple-element.40.parcel_ref), channel_id=1, source_target_pairs={{8,16},{24,32},{40,48},{56,64},{72,80},{88,96},{104,112},{120,128}... | collective-permute-start | bytes 884744 | tf_op jit(solution)/shard_map/ppermute | solution.py:367
  10.5 0.1 collective-permute-start
  10.6 2.7 %collective-permute-start.3 = (bf16[128,1024]{1,0:T(8,128)(2,1)S(1)}, bf16[128,1024]{1,0:T(8,128)(2,1)S(1)}, u32[]{:S(2)}, u32[]{:S(2)}) collective-permute-start(bf16[128,1024]{1,0:T(8,128)(2,1)S(1)} %collective-permute-done.2.refs_1_), channel_id=1, source_target_pairs={{0,1},{1,2},{2,3},{3,4},{4,5},{5,6},{6,7},{7,0},{8,15},{9,8},{10,9... | collective-permute-start | bytes 786440 | tf_op jit(solution)/shard_map/ppermute | solution.py:370
  13.2 1.7 %project.5 = (bf16[1,128,1024]{2,1,0:T(8,128)(2,1)S(1)}, bf16[256,1024]{1,0:T(8,128)(2,1)S(1)}, bf16[1024,256]{1,0:T(8,128)(2,1)S(1)}) custom-call(bf16[128,1024]{1,0:T(8,128)(2,1)S(1)} %copy-done, bf16[128,1024]{1,0:T(8,128)(2,1)S(1)} %collective-permute-done.2.refs_1_, f32[1,1024]{1,0:T(1,128)S(1)} %bitcast.2, ...), custom_call_target="tpu_custom_call" | custom-call | flops 1073741824 | bytes 5242880 | tf_op jit(solution)/shard_map/project/pallas_call | solution.py:152
  15.0 0.0 collective-permute-done.5.refs_0_
  15.0 0.1 collective-permute-start.7
  15.1 1.5 %collective-permute-done.1.cross_ref = bf16[144,1024]{1,0:T(8,128)(2,1)S(1)} collective-permute-done((bf16[144,1024]{1,0:T(8,128)(2,1)S(1)}, bf16[144,1024]{1,0:T(8,128)(2,1)S(1)}, u32[]{:S(2)}, u32[]{:S(2)}) %collective-permute-start.1) | collective-permute-done | bytes 294944 | tf_op jit(solution)/shard_map/ppermute | solution.py:367
  16.6 1.0 %project_near.1 = (bf16[2,128,1024]{2,1,0:T(8,128)(2,1)S(1)}, f32[8,128]{1,0:T(8,128)S(1)}) custom-call(bf16[144,1024]{1,0:T(8,128)(2,1)S(1)} %collective-permute-done.core_ref, bf16[144,1024]{1,0:T(8,128)(2,1)S(1)} %collective-permute-done.1.cross_ref, bf16[144,1024]{1,0:T(8,128)(2,1)S(1)} %get-tuple-element.40.parcel_ref, f32[1,1024]{1,0:T(1,128)S(1)} %bitcast.3, ...), custom_call_target="tpu_custom_call" | custom-call | flops 536870912 | bytes 4194304 | tf_op jit(solution)/shard_map/project_near/pallas_call | solution.py:112
  17.5 0.9 %collective-permute-done.3.refs_1_ = bf16[128,1024]{1,0:T(8,128)(2,1)S(1)} collective-permute-done((bf16[128,1024]{1,0:T(8,128)(2,1)S(1)}, bf16[128,1024]{1,0:T(8,128)(2,1)S(1)}, u32[]{:S(2)}, u32[]{:S(2)}) %collective-permute-start.3) | collective-permute-done | bytes 262176 | tf_op jit(solution)/shard_map/ppermute | solution.py:370
  18.5 3.4 %collective-permute-start.4 = (bf16[128,1024]{1,0:T(8,128)(2,1)S(1)}, bf16[128,1024]{1,0:T(8,128)(2,1)S(1)}, u32[]{:S(2)}, u32[]{:S(2)}) collective-permute-start(bf16[128,1024]{1,0:T(8,128)(2,1)S(1)} %collective-permute-done.3.refs_1_), channel_id=1, source_target_pairs={{0,1},{1,2},{2,3},{3,4},{4,5},{5,6},{6,7},{7,0},{8,15},{9,8},{10,9... | collective-permute-start | bytes 786440 | tf_op jit(solution)/shard_map/ppermute | solution.py:377
  21.9 1.5 %project.6 = (bf16[256,1024]{1,0:T(8,128)(2,1)S(1)}, bf16[1024,256]{1,0:T(8,128)(2,1)S(1)}) custom-call(bf16[128,1024]{1,0:T(8,128)(2,1)S(1)} %collective-permute-done.5.refs_0_, bf16[128,1024]{1,0:T(8,128)(2,1)S(1)} %collective-permute-done.3.refs_1_, f32[1,1024]{1,0:T(1,128)S(1)} %bitcast.4, bf16[1024,2048]{1,0:T(8,128)(2,1)S(1)} %get-tuple-element.46.refs_4_.refs_3_.refs_2_), custom_call_target="tpu_custom_call" | custom-call | flops 1073741824 | bytes 5242880 | tf_op jit(solution)/shard_map/project/pallas_call | solution.py:152
  23.4 0.6 %collective-permute-done.7.refs_0_ = bf16[128,1024]{1,0:T(8,128)(2,1)S(1)} collective-permute-done((bf16[128,1024]{1,0:T(8,128)(2,1)S(1)}, bf16[128,1024]{1,0:T(8,128)(2,1)S(1)}, u32[]{:S(2)}, u32[]{:S(2)}) %collective-permute-start.7) | collective-permute-done | bytes 262176 | tf_op jit(solution)/shard_map/ppermute | solution.py:372
  24.0 0.0 collective-permute-start.8
  24.0 0.2 attend.4
  24.1 4.0 %collective-permute-done.4.refs_1_ = bf16[128,1024]{1,0:T(8,128)(2,1)S(1)} collective-permute-done((bf16[128,1024]{1,0:T(8,128)(2,1)S(1)}, bf16[128,1024]{1,0:T(8,128)(2,1)S(1)}, u32[]{:S(2)}, u32[]{:S(2)}) %collective-permute-start.4) | collective-permute-done | bytes 262176 | tf_op jit(solution)/shard_map/ppermute | solution.py:377
  28.1 3.7 %collective-permute-start.6 = (bf16[128,1024]{1,0:T(8,128)(2,1)S(1)}, bf16[128,1024]{1,0:T(8,128)(2,1)S(1)}, u32[]{:S(2)}, u32[]{:S(2)}) collective-permute-start(bf16[128,1024]{1,0:T(8,128)(2,1)S(1)} %collective-permute-done.4.refs_1_), channel_id=1, source_target_pairs={{0,1},{1,2},{2,3},{3,4},{4,5},{5,6},{6,7},{7,0},{8,15},{9,8},{10,9... | collective-permute-start | bytes 786440 | tf_op jit(solution)/shard_map/ppermute | solution.py:383
  31.8 2.3 %collective-permute-done.8.refs_0_ = bf16[128,1024]{1,0:T(8,128)(2,1)S(1)} collective-permute-done((bf16[128,1024]{1,0:T(8,128)(2,1)S(1)}, bf16[128,1024]{1,0:T(8,128)(2,1)S(1)}, u32[]{:S(2)}, u32[]{:S(2)}) %collective-permute-start.8) | collective-permute-done | bytes 262176 | tf_op jit(solution)/shard_map/ppermute | solution.py:379
  34.1 0.9 %project.8 = (bf16[128,1024]{1,0:T(8,128)(2,1)S(1)}, bf16[1024,128]{1,0:T(8,128)(2,1)S(1)}) custom-call(bf16[128,1024]{1,0:T(8,128)(2,1)S(1)} %collective-permute-done.8.refs_0_, f32[1,1024]{1,0:T(1,128)S(1)} %bitcast.5, bf16[1024,2048]{1,0:T(8,128)(2,1)S(1)} %get-tuple-element.46.refs_4_.refs_3_.refs_2_), custom_call_target="tpu_custom_call" | custom-call | flops 536870912 | bytes 5242880 | tf_op jit(solution)/shard_map/project/pallas_call | solution.py:152
  35.0 1.5 %project.7 = (bf16[256,1024]{1,0:T(8,128)(2,1)S(1)}, bf16[1024,256]{1,0:T(8,128)(2,1)S(1)}) custom-call(bf16[128,1024]{1,0:T(8,128)(2,1)S(1)} %collective-permute-done.7.refs_0_, bf16[128,1024]{1,0:T(8,128)(2,1)S(1)} %collective-permute-done.4.refs_1_, f32[1,1024]{1,0:T(1,128)S(1)} %bitcast.6, bf16[1024,2048]{1,0:T(8,128)(2,1)S(1)} %get-tuple-element.46.refs_4_.refs_3_.refs_2_), custom_call_target="tpu_custom_call" | custom-call | flops 1073741824 | bytes 5242880 | tf_op jit(solution)/shard_map/project/pallas_call | solution.py:152
  36.5 0.8 %attend.5 = (f32[1,8,256]{2,1,0:T(8,128)S(1)}, f32[1,8,256]{2,1,0:T(8,128)S(1)}, f32[1,1024,128]{2,1,0:T(8,128)S(1)}) custom-call(f32[8,128]{1,0:T(8,128)S(1)} %get-tuple-element.69.refs_0_, bf16[2,128,1024]{2,1,0:T(8,128)(2,1)S(1)} %get-tuple-element.43.refs_1_.refs_2_, ...), custom_call_target="tpu_custom_call", output_to_operand_aliasing={{0}: (6, {}), {1}: (7, {}), {2}: (8, {})} | custom-call | flops 536870912 | bytes 4194304 | tf_op jit(solution)/shard_map/attend/pallas_call | solution.py:254
  37.3 0.0 collective-permute-done.6.refs_0_
  37.3 0.9 %project.9 = (bf16[128,1024]{1,0:T(8,128)(2,1)S(1)}, bf16[1024,128]{1,0:T(8,128)(2,1)S(1)}) custom-call(bf16[128,1024]{1,0:T(8,128)(2,1)S(1)} %collective-permute-done.6.refs_0_, f32[1,1024]{1,0:T(1,128)S(1)} %bitcast.7, bf16[1024,2048]{1,0:T(8,128)(2,1)S(1)} %get-tuple-element.46.refs_4_.refs_3_.refs_2_), custom_call_target="tpu_custom_call" | custom-call | flops 536870912 | bytes 5242880 | tf_op jit(solution)/shard_map/project/pallas_call | solution.py:152
  38.2 0.0 copy-start.1
  38.2 0.2 attend.6
  38.3 2.1 %collective-permute-start.9 = (bf16[1088,128]{1,0:T(8,128)(2,1)S(1)}, bf16[1088,128]{1,0:T(8,128)(2,1)S(1)}, u32[]{:S(2)}, u32[]{:S(2)}) collective-permute-start(bf16[1088,128]{1,0:T(8,128)(2,1)S(1)} %get-tuple-element.68), channel_id=1, source_target_pairs={{8,16},{24,32},{40,48},{56,64},{72,80},{88,96},{104,112},{120,128}... | collective-permute-start | bytes 835592 | tf_op jit(solution)/shard_map/ppermute | solution.py:390
  40.4 2.3 %attend.7 = (f32[2,8,256]{2,1,0:T(8,128)S(1)}, f32[2,8,256]{2,1,0:T(8,128)S(1)}, f32[2,1024,128]{2,1,0:T(8,128)S(1)}, bf16[1088,128]{1,0:T(8,128)(2,1)S(1)}) custom-call(f32[8,128]{1,0:T(8,128)S(1)} %get-tuple-element.69.refs_0_, bf16[1,128,1024]{2,1,0:T(8,128)(2,1)S(1)} %get-tuple-element.70.refs_1_, ...), custom_call_target="tpu_custom_call" | custom-call | flops 1342177280 | bytes 4194304 | tf_op jit(solution)/shard_map/attend/pallas_call | solution.py:254
  42.7 1.6 %collective-permute-start.10 = (bf16[1088,128]{1,0:T(8,128)(2,1)S(1)}, bf16[1088,128]{1,0:T(8,128)(2,1)S(1)}, u32[]{:S(2)}, u32[]{:S(2)}) collective-permute-start(bf16[1088,128]{1,0:T(8,128)(2,1)S(1)} %get-tuple-element.74), channel_id=1, source_target_pairs={{0,8},{8,0},{16,24},{24,16},{32,40},{40,32},{48,56},{56,48},{64,72... | collective-permute-start | bytes 835592 | tf_op jit(solution)/shard_map/ppermute | solution.py:394
  44.3 4.1 %collective-permute-done.9.cross_ref = bf16[1088,128]{1,0:T(8,128)(2,1)S(1)} collective-permute-done((bf16[1088,128]{1,0:T(8,128)(2,1)S(1)}, bf16[1088,128]{1,0:T(8,128)(2,1)S(1)}, u32[]{:S(2)}, u32[]{:S(2)}) %collective-permute-start.9) | collective-permute-done | bytes 278560 | tf_op jit(solution)/shard_map/ppermute | solution.py:390
  48.5 1.2 %finish.1 = bf16[128,1024]{1,0:T(8,128)(2,1)} custom-call(f32[2,16,128]{2,1,0:T(8,128)S(1)} %finish_first.1.lse_ref, f32[2,8,256]{2,1,0:T(8,128)S(1)} %get-tuple-element.72.l_ref, f32[2,1024,128]{2,1,0:T(8,128)S(1)} %get-tuple-element.73.own_ref, bf16[1088,128]{1,0:T(8,128)(2,1)S(1)} %collective-permute-done.10.core_ref, ...), custom_call_target="tpu_custom_call" | custom-call | flops 268435456 | bytes 4194304 | tf_op jit(solution)/shard_map/finish/pallas_call | solution.py:328
  (9 shorter events, 0.0 us)
Async XLA Ops:
  0.0 6.3 %copy-start = (bf16[128,1024]{1,0:T(8,128)(2,1)S(1)}, bf16[128,1024]{1,0:T(8,128)(2,1)}, u32[]{:S(2)}) copy-start(bf16[128,1024]{1,0:T(8,128)(2,1)} %features_ref.3) | copy-start | bytes 786436
  0.0 13.2 %copy-start.2 = (f32[1024]{0:T(1024)S(1)}, f32[1024]{0:T(1024)}, u32[]{:S(2)}) copy-start(f32[1024]{0:T(1024)} %param.7) | copy-start | bytes 12292
  0.0 10.6 %collective-permute-start.2 = (bf16[128,1024]{1,0:T(8,128)(2,1)}, bf16[128,1024]{1,0:T(8,128)(2,1)S(1)}, u32[]{:S(2)}, u32[]{:S(2)}) collective-permute-start(bf16[128,1024]{1,0:T(8,128)(2,1)} %features_ref.3), channel_id=1, source_target_pairs={{0,1},{1,2},{2,3},{3,4},{4,5},{5,6},{6,7},{7,0},{8,15},{9,8},{10,9... | collective-permute-start | bytes 786440 | tf_op jit(solution)/shard_map/ppermute | solution.py:364
  6.3 8.7 %collective-permute-start.5 = (bf16[128,1024]{1,0:T(8,128)(2,1)S(1)}, bf16[128,1024]{1,0:T(8,128)(2,1)S(1)}, u32[]{:S(2)}, u32[]{:S(2)}) collective-permute-start(bf16[128,1024]{1,0:T(8,128)(2,1)S(1)} %copy-done), channel_id=1, source_target_pairs={{1,0},{2,1},{3,2},{4,3},{5,4},{6,5},{7,6},{0,7},{15,8},{8,9},{9,10... | collective-permute-start | bytes 786440 | tf_op jit(solution)/shard_map/ppermute | solution.py:366
  6.4 10.2 %collective-permute-start.1 = (bf16[144,1024]{1,0:T(8,128)(2,1)S(1)}, bf16[144,1024]{1,0:T(8,128)(2,1)S(1)}, u32[]{:S(2)}, u32[]{:S(2)}) collective-permute-start(bf16[144,1024]{1,0:T(8,128)(2,1)S(1)} %get-tuple-element.40.parcel_ref), channel_id=1, source_target_pairs={{8,16},{24,32},{40,48},{56,64},{72,80},{88,96},{104,112},{120,128}... | collective-permute-start | bytes 884744 | tf_op jit(solution)/shard_map/ppermute | solution.py:367
  10.5 6.1 %collective-permute-start = (bf16[144,1024]{1,0:T(8,128)(2,1)S(1)}, bf16[144,1024]{1,0:T(8,128)(2,1)S(1)}, u32[]{:S(2)}, u32[]{:S(2)}) collective-permute-start(bf16[144,1024]{1,0:T(8,128)(2,1)S(1)} %get-tuple-element.40.parcel_ref), channel_id=1, source_target_pairs={{0,8},{8,0},{16,24},{24,16},{32,40},{40,32},{48,56},{56,48},{64,72... | collective-permute-start | bytes 884744 | tf_op jit(solution)/shard_map/ppermute | solution.py:368
  10.6 7.9 %collective-permute-start.3 = (bf16[128,1024]{1,0:T(8,128)(2,1)S(1)}, bf16[128,1024]{1,0:T(8,128)(2,1)S(1)}, u32[]{:S(2)}, u32[]{:S(2)}) collective-permute-start(bf16[128,1024]{1,0:T(8,128)(2,1)S(1)} %collective-permute-done.2.refs_1_), channel_id=1, source_target_pairs={{0,1},{1,2},{2,3},{3,4},{4,5},{5,6},{6,7},{7,0},{8,15},{9,8},{10,9... | collective-permute-start | bytes 786440 | tf_op jit(solution)/shard_map/ppermute | solution.py:370
  15.0 9.0 %collective-permute-start.7 = (bf16[128,1024]{1,0:T(8,128)(2,1)S(1)}, bf16[128,1024]{1,0:T(8,128)(2,1)S(1)}, u32[]{:S(2)}, u32[]{:S(2)}) collective-permute-start(bf16[128,1024]{1,0:T(8,128)(2,1)S(1)} %collective-permute-done.5.refs_0_), channel_id=1, source_target_pairs={{1,0},{2,1},{3,2},{4,3},{5,4},{6,5},{7,6},{0,7},{15,8},{8,9},{9,10... | collective-permute-start | bytes 786440 | tf_op jit(solution)/shard_map/ppermute | solution.py:372
  18.5 9.6 %collective-permute-start.4 = (bf16[128,1024]{1,0:T(8,128)(2,1)S(1)}, bf16[128,1024]{1,0:T(8,128)(2,1)S(1)}, u32[]{:S(2)}, u32[]{:S(2)}) collective-permute-start(bf16[128,1024]{1,0:T(8,128)(2,1)S(1)} %collective-permute-done.3.refs_1_), channel_id=1, source_target_pairs={{0,1},{1,2},{2,3},{3,4},{4,5},{5,6},{6,7},{7,0},{8,15},{9,8},{10,9... | collective-permute-start | bytes 786440 | tf_op jit(solution)/shard_map/ppermute | solution.py:377
  24.0 10.1 %collective-permute-start.8 = (bf16[128,1024]{1,0:T(8,128)(2,1)S(1)}, bf16[128,1024]{1,0:T(8,128)(2,1)S(1)}, u32[]{:S(2)}, u32[]{:S(2)}) collective-permute-start(bf16[128,1024]{1,0:T(8,128)(2,1)S(1)} %collective-permute-done.7.refs_0_), channel_id=1, source_target_pairs={{1,0},{2,1},{3,2},{4,3},{5,4},{6,5},{7,6},{0,7},{15,8},{8,9},{9,10... | collective-permute-start | bytes 786440 | tf_op jit(solution)/shard_map/ppermute | solution.py:379
  28.1 9.1 %collective-permute-start.6 = (bf16[128,1024]{1,0:T(8,128)(2,1)S(1)}, bf16[128,1024]{1,0:T(8,128)(2,1)S(1)}, u32[]{:S(2)}, u32[]{:S(2)}) collective-permute-start(bf16[128,1024]{1,0:T(8,128)(2,1)S(1)} %collective-permute-done.4.refs_1_), channel_id=1, source_target_pairs={{0,1},{1,2},{2,3},{3,4},{4,5},{5,6},{6,7},{7,0},{8,15},{9,8},{10,9... | collective-permute-start | bytes 786440 | tf_op jit(solution)/shard_map/ppermute | solution.py:383
  38.2 10.3 %copy-start.1 = (bf16[1024,1024]{1,0:T(8,128)(2,1)S(1)}, bf16[1024,1024]{1,0:T(8,128)(2,1)}, u32[]{:S(2)}) copy-start(bf16[1024,1024]{1,0:T(8,128)(2,1)} %w_ref.3) | copy-start | bytes 6291460
  38.3 10.1 %collective-permute-start.9 = (bf16[1088,128]{1,0:T(8,128)(2,1)S(1)}, bf16[1088,128]{1,0:T(8,128)(2,1)S(1)}, u32[]{:S(2)}, u32[]{:S(2)}) collective-permute-start(bf16[1088,128]{1,0:T(8,128)(2,1)S(1)} %get-tuple-element.68), channel_id=1, source_target_pairs={{8,16},{24,32},{40,48},{56,64},{72,80},{88,96},{104,112},{120,128}... | collective-permute-start | bytes 835592 | tf_op jit(solution)/shard_map/ppermute | solution.py:390
  42.7 5.8 %collective-permute-start.10 = (bf16[1088,128]{1,0:T(8,128)(2,1)S(1)}, bf16[1088,128]{1,0:T(8,128)(2,1)S(1)}, u32[]{:S(2)}, u32[]{:S(2)}) collective-permute-start(bf16[1088,128]{1,0:T(8,128)(2,1)S(1)} %get-tuple-element.74), channel_id=1, source_target_pairs={{0,8},{8,0},{16,24},{24,16},{32,40},{40,32},{48,56},{56,48},{64,72... | collective-permute-start | bytes 835592 | tf_op jit(solution)/shard_map/ppermute | solution.py:394

commit v2 on v1

--- a/solution.py
+++ b/solution.py
@@ -90,31 +90,32 @@
             q_ref[n, :, c * 512 + j * 128 : c * 512 + (j + 1) * 128] = turned.astype(jnp.bfloat16)
 
 
-def near_kernel(core_ref, cross_ref, parcel_ref, gain_ref, w_ref, q_ref, info_ref):
+def needed(ref, n):
     here, group = lax.axis_index("head"), lax.axis_index("dom")
     row = lax.broadcasted_iota(jnp.int32, (16, 128), 0)
     lane = lax.broadcasted_iota(jnp.int32, (16, 128), 1)
-    info = jnp.zeros((1, 1), jnp.float32)
-    for n, ref in enumerate((parcel_ref, core_ref, cross_ref)):
-        if n > 0:
-            project_queries(normed(ref[:TILE], gain_ref[...]), w_ref, q_ref, n - 1)
-        lists = ref[pl.ds(TILE, 16), :128].astype(jnp.float32).astype(jnp.int32)
-        count = jnp.where((row == NB) & (lane == here), lists, 0).astype(jnp.float32)
-        count = jnp.sum(jnp.sum(count, axis=0, keepdims=True), axis=1, keepdims=True)
-        used = (row == here) & (lane < jnp.minimum(count, NB).astype(jnp.int32))
-        used = used & (jnp.right_shift(lists, 3) == group)
-        bits = jnp.where(used, jnp.left_shift(1, (lists & (NB - 1)) + n * NB), 0).astype(jnp.float32)
-        info = info + jnp.sum(jnp.sum(bits, axis=0, keepdims=True), axis=1, keepdims=True)
+    lists = ref[pl.ds(TILE, 16), :128].astype(jnp.float32).astype(jnp.int32)
+    count = jnp.where((row == NB) & (lane == here), lists, 0).astype(jnp.float32)
+    count = jnp.sum(jnp.sum(count, axis=0, keepdims=True), axis=1, keepdims=True)
+    used = (row == here) & (lane < jnp.minimum(count, NB).astype(jnp.int32))
+    used = used & (jnp.right_shift(lists, 3) == group)
+    bits = jnp.where(used, jnp.left_shift(1, (lists & (NB - 1)) + n * NB), 0).astype(jnp.float32)
+    return jnp.sum(jnp.sum(bits, axis=0, keepdims=True), axis=1, keepdims=True)
+
+
+def near_kernel(core_ref, parcel_ref, gain_ref, w_ref, q_ref, info_ref):
+    project_queries(normed(core_ref[:TILE], gain_ref[...]), w_ref, q_ref, 0)
+    info = needed(parcel_ref, 0) + needed(core_ref, 1)
     info_ref[...] = jnp.broadcast_to(info, info_ref.shape)
 
 
-def project_near(core, cross, parcel, gain, w_query):
+def project_near(core, parcel, gain, w_query):
     return pl.pallas_call(
         near_kernel,
-        in_specs=[VMEM] * 5,
+        in_specs=[VMEM] * 4,
         out_specs=[VMEM] * 2,
         out_shape=[
-            jax.ShapeDtypeStruct((2, TILE, D), jnp.bfloat16),
+            jax.ShapeDtypeStruct((1, TILE, D), jnp.bfloat16),
             jax.ShapeDtypeStruct((8, 128), jnp.float32),
         ],
         compiler_params=PARAMS,
@@ -122,7 +123,29 @@
             flops=4 * TILE * D * D, bytes_accessed=4 * 1024 * 1024, transcendentals=0
         ),
         name="project_near",
-    )(core, cross, parcel, gain, w_query)
+    )(core, parcel, gain, w_query)
+
+
+def later_kernel(cross_ref, gain_ref, w_ref, info_in, q_ref, info_ref):
+    project_queries(normed(cross_ref[:TILE], gain_ref[...]), w_ref, q_ref, 0)
+    info_ref[...] = info_in[...] + jnp.broadcast_to(needed(cross_ref, 2), info_ref.shape)
+
+
+def project_later(cross, gain, w_query, info):
+    return pl.pallas_call(
+        later_kernel,
+        in_specs=[VMEM] * 4,
+        out_specs=[VMEM] * 2,
+        out_shape=[
+            jax.ShapeDtypeStruct((1, TILE, D), jnp.bfloat16),
+            jax.ShapeDtypeStruct((8, 128), jnp.float32),
+        ],
+        compiler_params=PARAMS,
+        cost_estimate=pl.CostEstimate(
+            flops=2 * TILE * D * D, bytes_accessed=3 * 1024 * 1024, transcendentals=0
+        ),
+        name="project_later",
+    )(cross, gain, w_query, info)
 
 
 def project_kernel(count, with_query, *refs):
@@ -364,32 +387,35 @@
     one = [lax.ppermute(features, *up)]
     parcel, w_query, w_kv = prepare(features, adjacency, counts.reshape(1, NB), in_proj)
     two = [lax.ppermute(tied(features, parcel), *down)]
-    from_cross = lax.ppermute(parcel, "dom", hop)
     from_core = lax.ppermute(parcel, "dom", swap)
 
     one.append(lax.ppermute(tied(one[0], w_query), *up))
     q_own, *kv_a = project([features, one[0]], gain, w_kv, w_query)
     two.append(lax.ppermute(tied(two[0], *kv_a), *down))
-    q_near, info = project_near(from_core, from_cross, parcel, gain, w_query)
+    from_row = lax.ppermute(tied(parcel, one[0]), "dom", hop)
+    q_core, info_core = project_near(from_core, parcel, gain, w_query)
     kv_a = ((0, -1), *kv_a)
-    pair, far = [(q_own, 0, 0), (q_near, 1, 0)], [(q_near, 2, 1)]
-
-    one.append(lax.ppermute(tied(one[1], q_near), *up))
+    pair = [(q_own, 0, 0), (q_core, 1, 0)]
+
+    one.append(lax.ppermute(tied(one[1], q_core), *up))
     kv_b = project([two[0], one[1]], gain, w_kv)
     two.append(lax.ppermute(tied(two[1], *kv_b), *down))
     kv_b = ((1, -2), *kv_b)
+    pair_state = attend(info_core, pair, [kv_a])
+    q_cross, info = project_later(from_row, gain, w_query, tied(info_core, *pair_state))
+    far = [(q_cross, 2, 0)]
+
+    one.append(lax.ppermute(tied(one[2], *pair_state), *up))
     far_state = attend(info, far, [kv_a, kv_b])
-
-    one.append(lax.ppermute(tied(one[2], *far_state), *up))
     kv_c = ((2, -3), *project([two[1], one[2]], gain, w_kv))
     kv_d = ((3,), *project([two[2]], gain, w_kv))
     far_state = attend(info, far, [kv_c, kv_d], far_state)
 
-    kv_e = ((4,), *project([tied(one[3], *far_state)], gain, w_kv))
+    kv_e = ((4,), *project([tied(one[3], *far_state, *pair_state)], gain, w_kv))
     *_, to_cross = attend(info, far, [kv_e], far_state, last=True)
     cross = lax.ppermute(to_cross, "dom", hop)
     *pair_state, to_core = attend(
-        tied(info, to_cross), pair, [kv_a, kv_b, kv_c, kv_d, kv_e], last=True
+        info, pair, [kv_b, kv_c, kv_d, kv_e], tied(pair_state, to_cross), last=True
     )
     core = lax.ppermute(to_core, "dom", swap)
     return finish(pair_state, core, cross, out_proj, features)

time: 50.7 us -> 49.2 us (0.970)
  Pallas kernels: 15.2 us -> 18.2 us
  waiting for transfers between devices: 13.4 us -> 10.5 us
  starting transfers between devices: 20.9 us -> 19.5 us
    ppermute x3, waiting for transfers between devices: 5.45 us -> 1.94 us  [the longest x1 1.94 us: body(): one.append(lax.ppermute(tied(one[1], q_core), *up))]
    ppermute x1, waiting for transfers between devices: 0.01 us -> 3.23 us  [body(): two = [lax.ppermute(tied(features, parcel), *down)]]
    pallas_call x4 -> x5, Pallas kernels: 3.39 us -> 6.08 us  [attend(): pl.pallas_call(functools.partial(attend_kernel, who, steps, not state, la...]
    ppermute x1, waiting for transfers between devices: 2.3 us -> 0.01 us  [body(): two.append(lax.ppermute(tied(two[1], *kv_b), *down))]
    ppermute x3, starting transfers between devices: 11.2 us -> 8.91 us  [the longest x1 3.69 us: body(): one.append(lax.ppermute(tied(one[2], *pair_state), *up))]
    ppermute x1, starting transfers between devices: 2.05 us -> 3.6 us  [body(): cross = lax.ppermute(to_cross, 'dom', hop)]
    ppermute x1, starting transfers between devices: 1.64 us -> 0.09 us  [body(): core = lax.ppermute(to_core, 'dom', swap)]
    ppermute x1, waiting for transfers between devices: 0.01 us -> 1.55 us  [body(): one = [lax.ppermute(features, *up)]]
  transfers between devices with their start and end apart: 11 -> 11, of which waited for: 6 -> 5; matrix products, arithmetic and copies ran while one was open for 0% -> 0% of each run, Pallas kernels for 26% -> 33%
where the time goes in v2:
time: 49.2 us; the launch traced here: 48.6 us
  starting transfers between devices  19.5 us (40%)
  Pallas kernels  18.2 us (37%)
  waiting for transfers between devices  10.5 us (21%)
    pallas_call x5, Pallas kernels, project(): pl.pallas_call(functools.partial(project_kernel, len(arrays), query), in_...  6.39 us
    pallas_call x5, Pallas kernels, attend(): pl.pallas_call(functools.partial(attend_kernel, who, steps, not state, la...  6.08 us
    ppermute x1, starting transfers between devices, body(): one.append(lax.ppermute(tied(one[2], *pair_state), *up))  3.69 us
    ppermute x1, starting transfers between devices, body(): cross = lax.ppermute(to_cross, 'dom', hop)  3.6 us
    ppermute x1, starting transfers between devices, body(): one.append(lax.ppermute(tied(one[0], w_query), *up))  3.59 us
    ppermute x1, waiting for transfers between devices, body(): cross = lax.ppermute(to_cross, 'dom', hop)  3.53 us
    ppermute x1, starting transfers between devices, body(): one.append(lax.ppermute(tied(one[1], q_core), *up))  3.31 us
    ppermute x1, waiting for transfers between devices, body(): two = [lax.ppermute(tied(features, parcel), *down)]  3.23 us
  transfers between devices with their start and end apart: 11, of which 5 were waited for; matrix products, arithmetic and copies ran while one was open for 0% of the time, Pallas kernels for 33%

profile of v2, /device:TPU:120, one launch (start us, length us, event | category | flops | bytes accessed | tf_op | source)
XLA Modules:
  0.0 48.6 jit_solution(4015588059301227377)
XLA Ops:
  0.0 3.1 %collective-permute-start = (bf16[128,1024]{1,0:T(8,128)(2,1)}, bf16[128,1024]{1,0:T(8,128)(2,1)S(1)}, u32[]{:S(2)}, u32[]{:S(2)}) collective-permute-start(bf16[128,1024]{1,0:T(8,128)(2,1)} %features_ref.3), channel_id=1, source_target_pairs={{0,1},{1,2},{2,3},{3,4},{4,5},{5,6},{6,7},{7,0},{8,15},{9,8},{10,9... | collective-permute-start | bytes 786440 | tf_op jit(solution)/shard_map/ppermute | solution.py:387
  3.1 3.2 %prepare.1 = (bf16[144,1024]{1,0:T(8,128)(2,1)S(1)}, bf16[1024,1024]{1,0:T(8,128)(2,1)S(1)}, bf16[1024,2048]{1,0:T(8,128)(2,1)S(1)}) custom-call(bf16[128,1024]{1,0:T(8,128)(2,1)} %features_ref.3, s32[8,8]{1,0:T(8,128)} %adjacency_ref.1, s32[1,8]{1,0:T(1,128)} %bitcast.9, bf16[1024,3072]{1,0:T(8,128)(2,1)} %w_ref.2), custom_call_target="tpu_custom_call" | custom-call | bytes 12582912 | tf_op jit(solution)/shard_map/prepare/pallas_call | solution.py:63
  6.3 0.1 collective-permute-start.3
  6.4 0.1 collective-permute-start.2
  6.5 1.5 %collective-permute-done.refs_1_ = bf16[128,1024]{1,0:T(8,128)(2,1)S(1)} collective-permute-done((bf16[128,1024]{1,0:T(8,128)(2,1)}, bf16[128,1024]{1,0:T(8,128)(2,1)S(1)}, u32[]{:S(2)}, u32[]{:S(2)}) %collective-permute-start) | collective-permute-done | bytes 262176 | tf_op jit(solution)/shard_map/ppermute | solution.py:387
  8.1 3.6 %collective-permute-start.4 = (bf16[128,1024]{1,0:T(8,128)(2,1)S(1)}, bf16[128,1024]{1,0:T(8,128)(2,1)S(1)}, u32[]{:S(2)}, u32[]{:S(2)}) collective-permute-start(bf16[128,1024]{1,0:T(8,128)(2,1)S(1)} %collective-permute-done.refs_1_), channel_id=1, source_target_pairs={{0,1},{1,2},{2,3},{3,4},{4,5},{5,6},{6,7},{7,0},{8,15},{9,8},{10,9... | collective-permute-start | bytes 786440 | tf_op jit(solution)/shard_map/ppermute | solution.py:392
  11.7 1.7 %project.5 = (bf16[1,128,1024]{2,1,0:T(8,128)(2,1)S(1)}, bf16[256,1024]{1,0:T(8,128)(2,1)S(1)}, bf16[1024,256]{1,0:T(8,128)(2,1)S(1)}) custom-call(bf16[128,1024]{1,0:T(8,128)(2,1)S(1)} %copy-done, bf16[128,1024]{1,0:T(8,128)(2,1)S(1)} %collective-permute-done.refs_1_, f32[1,1024]{1,0:T(1,128)S(1)} %bitcast.2, ...), custom_call_target="tpu_custom_call" | custom-call | flops 1073741824 | bytes 5242880 | tf_op jit(solution)/shard_map/project/pallas_call | solution.py:175
  13.4 3.2 %collective-permute-done.3.refs_0_ = bf16[128,1024]{1,0:T(8,128)(2,1)S(1)} collective-permute-done((bf16[128,1024]{1,0:T(8,128)(2,1)S(1)}, bf16[128,1024]{1,0:T(8,128)(2,1)S(1)}, u32[]{:S(2)}, u32[]{:S(2)}) %collective-permute-start.3) | collective-permute-done | bytes 262176 | tf_op jit(solution)/shard_map/ppermute | solution.py:389
  16.6 0.0 collective-permute-start.5
  16.6 1.9 %collective-permute-start.1 = (bf16[144,1024]{1,0:T(8,128)(2,1)S(1)}, bf16[144,1024]{1,0:T(8,128)(2,1)S(1)}, u32[]{:S(2)}, u32[]{:S(2)}) collective-permute-start(bf16[144,1024]{1,0:T(8,128)(2,1)S(1)} %get-tuple-element.50.parcel_ref), channel_id=1, source_target_pairs={{8,16},{24,32},{40,48},{56,64},{72,80},{88,96},{104,112},{120,128}... | collective-permute-start | bytes 884744 | tf_op jit(solution)/shard_map/ppermute | solution.py:395
  18.6 0.0 collective-permute-done.2.core_ref
  18.6 0.6 %project_near.1 = (bf16[1,128,1024]{2,1,0:T(8,128)(2,1)S(1)}, f32[8,128]{1,0:T(8,128)S(1)}) custom-call(bf16[144,1024]{1,0:T(8,128)(2,1)S(1)} %collective-permute-done.2.core_ref, bf16[144,1024]{1,0:T(8,128)(2,1)S(1)} %get-tuple-element.50.parcel_ref, f32[1,1024]{1,0:T(1,128)S(1)} %bitcast.3, bf16[1024,1024]{1,0:T(8,128)(2,1)S(1)} %get-tuple-element.51.w_ref.refs_3_), custom_call_target="tpu_custom_call" | custom-call | flops 536870912 | bytes 4194304 | tf_op jit(solution)/shard_map/project_near/pallas_call | solution.py:113
  19.2 0.0 collective-permute-done.4.refs_1_
  19.2 3.3 %collective-permute-start.6 = (bf16[128,1024]{1,0:T(8,128)(2,1)S(1)}, bf16[128,1024]{1,0:T(8,128)(2,1)S(1)}, u32[]{:S(2)}, u32[]{:S(2)}) collective-permute-start(bf16[128,1024]{1,0:T(8,128)(2,1)S(1)} %collective-permute-done.4.refs_1_), channel_id=1, source_target_pairs={{0,1},{1,2},{2,3},{3,4},{4,5},{5,6},{6,7},{7,0},{8,15},{9,8},{10,9... | collective-permute-start | bytes 786440 | tf_op jit(solution)/shard_map/ppermute | solution.py:400
  22.5 1.5 %project.6 = (bf16[256,1024]{1,0:T(8,128)(2,1)S(1)}, bf16[1024,256]{1,0:T(8,128)(2,1)S(1)}) custom-call(bf16[128,1024]{1,0:T(8,128)(2,1)S(1)} %collective-permute-done.3.refs_0_, bf16[128,1024]{1,0:T(8,128)(2,1)S(1)} %collective-permute-done.4.refs_1_, f32[1,1024]{1,0:T(1,128)S(1)} %bitcast.4, bf16[1024,2048]{1,0:T(8,128)(2,1)S(1)} %get-tuple-element.53.refs_4_.refs_3_.refs_2_), custom_call_target="tpu_custom_call" | custom-call | flops 1073741824 | bytes 5242880 | tf_op jit(solution)/shard_map/project/pallas_call | solution.py:175
  24.0 0.2 collective-permute-done.5.refs_0_
  24.2 0.8 %attend.5 = (f32[2,8,256]{2,1,0:T(8,128)S(1)}, f32[2,8,256]{2,1,0:T(8,128)S(1)}, f32[2,1024,128]{2,1,0:T(8,128)S(1)}) custom-call(f32[8,128]{1,0:T(8,128)S(1)} %get-tuple-element.61.refs_0_.info_in, bf16[1,128,1024]{2,1,0:T(8,128)(2,1)S(1)} %get-tuple-element.54.refs_1_, bf16[1,128,1024]{2,1,0:T(8,128)(2,1)S(1)} %get-tuple-element.55.refs_2_, ...), custom_call_target="tpu_custom_call" | custom-call | flops 268435456 | bytes 4194304 | tf_op jit(solution)/shard_map/attend/pallas_call | solution.py:277
  25.0 1.9 %collective-permute-done.6.refs_1_ = bf16[128,1024]{1,0:T(8,128)(2,1)S(1)} collective-permute-done((bf16[128,1024]{1,0:T(8,128)(2,1)S(1)}, bf16[128,1024]{1,0:T(8,128)(2,1)S(1)}, u32[]{:S(2)}, u32[]{:S(2)}) %collective-permute-start.6) | collective-permute-done | bytes 262176 | tf_op jit(solution)/shard_map/ppermute | solution.py:400
  27.0 3.7 %collective-permute-start.8 = (bf16[128,1024]{1,0:T(8,128)(2,1)S(1)}, bf16[128,1024]{1,0:T(8,128)(2,1)S(1)}, u32[]{:S(2)}, u32[]{:S(2)}) collective-permute-start(bf16[128,1024]{1,0:T(8,128)(2,1)S(1)} %collective-permute-done.6.refs_1_), channel_id=1, source_target_pairs={{0,1},{1,2},{2,3},{3,4},{4,5},{5,6},{6,7},{7,0},{8,15},{9,8},{10,9... | collective-permute-start | bytes 786440 | tf_op jit(solution)/shard_map/ppermute | solution.py:408
  30.7 0.6 %project_later.1 = (bf16[1,128,1024]{2,1,0:T(8,128)(2,1)S(1)}, f32[8,128]{1,0:T(8,128)S(1)}) custom-call(bf16[144,1024]{1,0:T(8,128)(2,1)S(1)} %collective-permute-done.1.cross_ref, f32[1,1024]{1,0:T(1,128)S(1)} %bitcast.5, bf16[1024,1024]{1,0:T(8,128)(2,1)S(1)} %get-tuple-element.51.w_ref.refs_3_, f32[8,128]{1,0:T(8,128)S(1)} %get-tuple-element.61.refs_0_.info_in), custom_call_target="tpu_custom_call" | custom-call | flops 268435456 | bytes 3145728 | tf_op jit(solution)/shard_map/project_later/pallas_call | solution.py:135
  31.3 0.8 %attend.6 = (f32[1,8,256]{2,1,0:T(8,128)S(1)}, f32[1,8,256]{2,1,0:T(8,128)S(1)}, f32[1,1024,128]{2,1,0:T(8,128)S(1)}) custom-call(f32[8,128]{1,0:T(8,128)S(1)} %get-tuple-element.62.refs_0_, bf16[1,128,1024]{2,1,0:T(8,128)(2,1)S(1)} %get-tuple-element.75.refs_1_, bf16[256,1024]{1,0:T(8,128)(2,1)S(1)} %get-tuple-element.56.refs_3_.refs_2_, ...), custom_call_target="tpu_custom_call" | custom-call | flops 536870912 | bytes 4194304 | tf_op jit(solution)/shard_map/attend/pallas_call | solution.py:277
  32.1 0.9 %project.8 = (bf16[128,1024]{1,0:T(8,128)(2,1)S(1)}, bf16[1024,128]{1,0:T(8,128)(2,1)S(1)}) custom-call(bf16[128,1024]{1,0:T(8,128)(2,1)S(1)} %collective-permute-done.7.refs_0_, f32[1,1024]{1,0:T(1,128)S(1)} %bitcast.6, bf16[1024,2048]{1,0:T(8,128)(2,1)S(1)} %get-tuple-element.53.refs_4_.refs_3_.refs_2_), custom_call_target="tpu_custom_call" | custom-call | flops 536870912 | bytes 5242880 | tf_op jit(solution)/shard_map/project/pallas_call | solution.py:175
  33.0 1.5 %project.7 = (bf16[256,1024]{1,0:T(8,128)(2,1)S(1)}, bf16[1024,256]{1,0:T(8,128)(2,1)S(1)}) custom-call(bf16[128,1024]{1,0:T(8,128)(2,1)S(1)} %collective-permute-done.5.refs_0_, bf16[128,1024]{1,0:T(8,128)(2,1)S(1)} %collective-permute-done.6.refs_1_, f32[1,1024]{1,0:T(1,128)S(1)} %bitcast.7, bf16[1024,2048]{1,0:T(8,128)(2,1)S(1)} %get-tuple-element.53.refs_4_.refs_3_.refs_2_), custom_call_target="tpu_custom_call" | custom-call | flops 1073741824 | bytes 5242880 | tf_op jit(solution)/shard_map/project/pallas_call | solution.py:175
  34.5 1.4 %attend.7 = (f32[1,8,256]{2,1,0:T(8,128)S(1)}, f32[1,8,256]{2,1,0:T(8,128)S(1)}, f32[1,1024,128]{2,1,0:T(8,128)S(1)}) custom-call(f32[8,128]{1,0:T(8,128)S(1)} %get-tuple-element.62.refs_0_, bf16[1,128,1024]{2,1,0:T(8,128)(2,1)S(1)} %get-tuple-element.75.refs_1_, ...), custom_call_target="tpu_custom_call", output_to_operand_aliasing={{0}: (6, {}), {1}: (7, {}), {2}: (8, {})} | custom-call | flops 536870912 | bytes 4194304 | tf_op jit(solution)/shard_map/attend/pallas_call | solution.py:277
  35.9 0.9 %project.9 = (bf16[128,1024]{1,0:T(8,128)(2,1)S(1)}, bf16[1024,128]{1,0:T(8,128)(2,1)S(1)}) custom-call(bf16[128,1024]{1,0:T(8,128)(2,1)S(1)} %collective-permute-done.8.refs_0_, f32[1,1024]{1,0:T(1,128)S(1)} %bitcast.8, bf16[1024,2048]{1,0:T(8,128)(2,1)S(1)} %get-tuple-element.53.refs_4_.refs_3_.refs_2_), custom_call_target="tpu_custom_call" | custom-call | flops 536870912 | bytes 5242880 | tf_op jit(solution)/shard_map/project/pallas_call | solution.py:175
  36.8 0.0 copy-start.1
  36.8 0.2 attend.8
  37.0 3.6 %collective-permute-start.9 = (bf16[1088,128]{1,0:T(8,128)(2,1)S(1)}, bf16[1088,128]{1,0:T(8,128)(2,1)S(1)}, u32[]{:S(2)}, u32[]{:S(2)}) collective-permute-start(bf16[1088,128]{1,0:T(8,128)(2,1)S(1)} %get-tuple-element.85), channel_id=1, source_target_pairs={{8,16},{24,32},{40,48},{56,64},{72,80},{88,96},{104,112},{120,128}... | collective-permute-start | bytes 835592 | tf_op jit(solution)/shard_map/ppermute | solution.py:416
  40.6 2.9 %attend.9 = (f32[2,8,256]{2,1,0:T(8,128)S(1)}, f32[2,8,256]{2,1,0:T(8,128)S(1)}, f32[2,1024,128]{2,1,0:T(8,128)S(1)}, bf16[1088,128]{1,0:T(8,128)(2,1)S(1)}) custom-call(f32[8,128]{1,0:T(8,128)S(1)} %get-tuple-element.62.refs_0_, bf16[1,128,1024]{2,1,0:T(8,128)(2,1)S(1)} %get-tuple-element.54.refs_1_, ...), custom_call_target="tpu_custom_call", output_to_operand_aliasing={{0}: (11, {}), {1}: (12, {}), {2}: (13, {})} | custom-call | flops 1073741824 | bytes 4194304 | tf_op jit(solution)/shard_map/attend/pallas_call | solution.py:277
  43.5 0.1 collective-permute-start.10
  43.6 3.5 %collective-permute-done.9.cross_ref = bf16[1088,128]{1,0:T(8,128)(2,1)S(1)} collective-permute-done((bf16[1088,128]{1,0:T(8,128)(2,1)S(1)}, bf16[1088,128]{1,0:T(8,128)(2,1)S(1)}, u32[]{:S(2)}, u32[]{:S(2)}) %collective-permute-start.9) | collective-permute-done | bytes 278560 | tf_op jit(solution)/shard_map/ppermute | solution.py:416
  47.1 1.3 %finish.1 = bf16[128,1024]{1,0:T(8,128)(2,1)} custom-call(f32[2,16,128]{2,1,0:T(8,128)S(1)} %finish_first.1.lse_ref, f32[2,8,256]{2,1,0:T(8,128)S(1)} %get-tuple-element.90.l_ref, f32[2,1024,128]{2,1,0:T(8,128)S(1)} %get-tuple-element.91.own_ref, bf16[1088,128]{1,0:T(8,128)(2,1)S(1)} %collective-permute-done.10.core_ref, ...), custom_call_target="tpu_custom_call" | custom-call | flops 268435456 | bytes 4194304 | tf_op jit(solution)/shard_map/finish/pallas_call | solution.py:351
  (11 shorter events, 0.0 us)
Async XLA Ops:
  0.0 6.3 %copy-start = (bf16[128,1024]{1,0:T(8,128)(2,1)S(1)}, bf16[128,1024]{1,0:T(8,128)(2,1)}, u32[]{:S(2)}) copy-start(bf16[128,1024]{1,0:T(8,128)(2,1)} %features_ref.3) | copy-start | bytes 786436
  0.0 11.7 %copy-start.2 = (f32[1024]{0:T(1024)S(1)}, f32[1024]{0:T(1024)}, u32[]{:S(2)}) copy-start(f32[1024]{0:T(1024)} %param.7) | copy-start | bytes 12292
  0.0 8.1 %collective-permute-start = (bf16[128,1024]{1,0:T(8,128)(2,1)}, bf16[128,1024]{1,0:T(8,128)(2,1)S(1)}, u32[]{:S(2)}, u32[]{:S(2)}) collective-permute-start(bf16[128,1024]{1,0:T(8,128)(2,1)} %features_ref.3), channel_id=1, source_target_pairs={{0,1},{1,2},{2,3},{3,4},{4,5},{5,6},{6,7},{7,0},{8,15},{9,8},{10,9... | collective-permute-start | bytes 786440 | tf_op jit(solution)/shard_map/ppermute | solution.py:387
  6.3 10.3 %collective-permute-start.3 = (bf16[128,1024]{1,0:T(8,128)(2,1)S(1)}, bf16[128,1024]{1,0:T(8,128)(2,1)S(1)}, u32[]{:S(2)}, u32[]{:S(2)}) collective-permute-start(bf16[128,1024]{1,0:T(8,128)(2,1)S(1)} %copy-done), channel_id=1, source_target_pairs={{1,0},{2,1},{3,2},{4,3},{5,4},{6,5},{7,6},{0,7},{15,8},{8,9},{9,10... | collective-permute-start | bytes 786440 | tf_op jit(solution)/shard_map/ppermute | solution.py:389
  6.4 12.1 %collective-permute-start.2 = (bf16[144,1024]{1,0:T(8,128)(2,1)S(1)}, bf16[144,1024]{1,0:T(8,128)(2,1)S(1)}, u32[]{:S(2)}, u32[]{:S(2)}) collective-permute-start(bf16[144,1024]{1,0:T(8,128)(2,1)S(1)} %get-tuple-element.50.parcel_ref), channel_id=1, source_target_pairs={{0,8},{8,0},{16,24},{24,16},{32,40},{40,32},{48,56},{56,48},{64,72... | collective-permute-start | bytes 884744 | tf_op jit(solution)/shard_map/ppermute | solution.py:390
  8.1 11.1 %collective-permute-start.4 = (bf16[128,1024]{1,0:T(8,128)(2,1)S(1)}, bf16[128,1024]{1,0:T(8,128)(2,1)S(1)}, u32[]{:S(2)}, u32[]{:S(2)}) collective-permute-start(bf16[128,1024]{1,0:T(8,128)(2,1)S(1)} %collective-permute-done.refs_1_), channel_id=1, source_target_pairs={{0,1},{1,2},{2,3},{3,4},{4,5},{5,6},{6,7},{7,0},{8,15},{9,8},{10,9... | collective-permute-start | bytes 786440 | tf_op jit(solution)/shard_map/ppermute | solution.py:392
  16.6 7.6 %collective-permute-start.5 = (bf16[128,1024]{1,0:T(8,128)(2,1)S(1)}, bf16[128,1024]{1,0:T(8,128)(2,1)S(1)}, u32[]{:S(2)}, u32[]{:S(2)}) collective-permute-start(bf16[128,1024]{1,0:T(8,128)(2,1)S(1)} %collective-permute-done.3.refs_0_), channel_id=1, source_target_pairs={{1,0},{2,1},{3,2},{4,3},{5,4},{6,5},{7,6},{0,7},{15,8},{8,9},{9,10... | collective-permute-start | bytes 786440 | tf_op jit(solution)/shard_map/ppermute | solution.py:394
  16.6 14.0 %collective-permute-start.1 = (bf16[144,1024]{1,0:T(8,128)(2,1)S(1)}, bf16[144,1024]{1,0:T(8,128)(2,1)S(1)}, u32[]{:S(2)}, u32[]{:S(2)}) collective-permute-start(bf16[144,1024]{1,0:T(8,128)(2,1)S(1)} %get-tuple-element.50.parcel_ref), channel_id=1, source_target_pairs={{8,16},{24,32},{40,48},{56,64},{72,80},{88,96},{104,112},{120,128}... | collective-permute-start | bytes 884744 | tf_op jit(solution)/shard_map/ppermute | solution.py:395
  19.2 7.8 %collective-permute-start.6 = (bf16[128,1024]{1,0:T(8,128)(2,1)S(1)}, bf16[128,1024]{1,0:T(8,128)(2,1)S(1)}, u32[]{:S(2)}, u32[]{:S(2)}) collective-permute-start(bf16[128,1024]{1,0:T(8,128)(2,1)S(1)} %collective-permute-done.4.refs_1_), channel_id=1, source_target_pairs={{0,1},{1,2},{2,3},{3,4},{4,5},{5,6},{6,7},{7,0},{8,15},{9,8},{10,9... | collective-permute-start | bytes 786440 | tf_op jit(solution)/shard_map/ppermute | solution.py:400
  24.2 7.9 %collective-permute-start.7 = (bf16[128,1024]{1,0:T(8,128)(2,1)S(1)}, bf16[128,1024]{1,0:T(8,128)(2,1)S(1)}, u32[]{:S(2)}, u32[]{:S(2)}) collective-permute-start(bf16[128,1024]{1,0:T(8,128)(2,1)S(1)} %collective-permute-done.5.refs_0_), channel_id=1, source_target_pairs={{1,0},{2,1},{3,2},{4,3},{5,4},{6,5},{7,6},{0,7},{15,8},{8,9},{9,10... | collective-permute-start | bytes 786440 | tf_op jit(solution)/shard_map/ppermute | solution.py:402
  27.0 9.0 %collective-permute-start.8 = (bf16[128,1024]{1,0:T(8,128)(2,1)S(1)}, bf16[128,1024]{1,0:T(8,128)(2,1)S(1)}, u32[]{:S(2)}, u32[]{:S(2)}) collective-permute-start(bf16[128,1024]{1,0:T(8,128)(2,1)S(1)} %collective-permute-done.6.refs_1_), channel_id=1, source_target_pairs={{0,1},{1,2},{2,3},{3,4},{4,5},{5,6},{6,7},{7,0},{8,15},{9,8},{10,9... | collective-permute-start | bytes 786440 | tf_op jit(solution)/shard_map/ppermute | solution.py:408
  36.8 10.3 %copy-start.1 = (bf16[1024,1024]{1,0:T(8,128)(2,1)S(1)}, bf16[1024,1024]{1,0:T(8,128)(2,1)}, u32[]{:S(2)}) copy-start(bf16[1024,1024]{1,0:T(8,128)(2,1)} %w_ref.3) | copy-start | bytes 6291460
  37.0 10.1 %collective-permute-start.9 = (bf16[1088,128]{1,0:T(8,128)(2,1)S(1)}, bf16[1088,128]{1,0:T(8,128)(2,1)S(1)}, u32[]{:S(2)}, u32[]{:S(2)}) collective-permute-start(bf16[1088,128]{1,0:T(8,128)(2,1)S(1)} %get-tuple-element.85), channel_id=1, source_target_pairs={{8,16},{24,32},{40,48},{56,64},{72,80},{88,96},{104,112},{120,128}... | collective-permute-start | bytes 835592 | tf_op jit(solution)/shard_map/ppermute | solution.py:416
  43.5 3.6 %collective-permute-start.10 = (bf16[1088,128]{1,0:T(8,128)(2,1)S(1)}, bf16[1088,128]{1,0:T(8,128)(2,1)S(1)}, u32[]{:S(2)}, u32[]{:S(2)}) collective-permute-start(bf16[1088,128]{1,0:T(8,128)(2,1)S(1)} %get-tuple-element.92), channel_id=1, source_target_pairs={{0,8},{8,0},{16,24},{24,16},{32,40},{40,32},{48,56},{56,48},{64,72... | collective-permute-start | bytes 835592 | tf_op jit(solution)/shard_map/ppermute | solution.py:420

commit v3 on v2

--- a/solution.py
+++ b/solution.py
@@ -405,7 +405,7 @@
     q_cross, info = project_later(from_row, gain, w_query, tied(info_core, *pair_state))
     far = [(q_cross, 2, 0)]
 
-    one.append(lax.ppermute(tied(one[2], *pair_state), *up))
+    one.append(lax.ppermute(tied(one[2], kv_b[1]), *up))
     far_state = attend(info, far, [kv_a, kv_b])
     kv_c = ((2, -3), *project([two[1], one[2]], gain, w_kv))
     kv_d = ((3,), *project([two[2]], gain, w_kv))

time: 49.2 us -> 49.2 us (level)
  Pallas kernels: 18.2 us -> 16.9 us
  waiting for transfers between devices: 10.5 us -> 11.8 us
    ppermute x1, waiting for transfers between devices: 3.53 us -> 5.44 us  [body(): cross = lax.ppermute(to_cross, 'dom', hop)]
    pallas_call x5, Pallas kernels: 6.08 us -> 4.78 us  [attend(): pl.pallas_call(functools.partial(attend_kernel, who, steps, not state, la...]
    ppermute x1, waiting for transfers between devices: 1.94 us -> 1.29 us  [body(): one.append(lax.ppermute(tied(one[1], q_core), *up))]
    ppermute x1, starting transfers between devices: 0.09 us -> 0.65 us  [body(): core = lax.ppermute(to_core, 'dom', swap)]
    ppermute x1, starting transfers between devices: 3.6 us -> 3.09 us  [body(): cross = lax.ppermute(to_cross, 'dom', hop)]
  transfers between devices with their start and end apart: 11 -> 11, of which waited for: 5 -> 5; matrix products, arithmetic and copies ran while one was open for 0% -> 0% of each run, Pallas kernels for 33% -> 30%
where the time goes in v3:
time: 49.2 us; the launch traced here: 48.6 us
  starting transfers between devices  19.5 us (40%)
  Pallas kernels  16.9 us (34%)
  waiting for transfers between devices  11.8 us (24%)
    pallas_call x5, Pallas kernels, project(): pl.pallas_call(functools.partial(project_kernel, len(arrays), query), in_...  6.39 us
    ppermute x1, waiting for transfers between devices, body(): cross = lax.ppermute(to_cross, 'dom', hop)  5.44 us
    pallas_call x5, Pallas kernels, attend(): pl.pallas_call(functools.partial(attend_kernel, who, steps, not state, la...  4.78 us
    ppermute x1, starting transfers between devices, body(): one.append(lax.ppermute(tied(one[2], kv_b[1]), *up))  3.69 us
    ppermute x1, starting transfers between devices, body(): one.append(lax.ppermute(tied(one[0], w_query), *up))  3.59 us
    ppermute x1, starting transfers between devices, body(): one.append(lax.ppermute(tied(one[1], q_core), *up))  3.31 us
    ppermute x1, waiting for transfers between devices, body(): two = [lax.ppermute(tied(features, parcel), *down)]  3.23 us
    pallas_call x1, Pallas kernels, prepare(): pl.pallas_call(prepare_kernel, in_specs=[pl.BlockSpec(memory_space=pltpu....  3.2 us
  transfers between devices with their start and end apart: 11, of which 5 were waited for; matrix products, arithmetic and copies ran while one was open for 0% of the time, Pallas kernels for 30%

profile of v3, /device:TPU:120, one launch (start us, length us, event | category | flops | bytes accessed | tf_op | source)
XLA Modules:
  0.0 48.6 jit_solution(4015588059301227377)
XLA Ops:
  0.0 3.1 %collective-permute-start = (bf16[128,1024]{1,0:T(8,128)(2,1)}, bf16[128,1024]{1,0:T(8,128)(2,1)S(1)}, u32[]{:S(2)}, u32[]{:S(2)}) collective-permute-start(bf16[128,1024]{1,0:T(8,128)(2,1)} %features_ref.3), channel_id=1, source_target_pairs={{0,1},{1,2},{2,3},{3,4},{4,5},{5,6},{6,7},{7,0},{8,15},{9,8},{10,9... | collective-permute-start | bytes 786440 | tf_op jit(solution)/shard_map/ppermute | solution.py:387
  3.1 3.2 %prepare.1 = (bf16[144,1024]{1,0:T(8,128)(2,1)S(1)}, bf16[1024,1024]{1,0:T(8,128)(2,1)S(1)}, bf16[1024,2048]{1,0:T(8,128)(2,1)S(1)}) custom-call(bf16[128,1024]{1,0:T(8,128)(2,1)} %features_ref.3, s32[8,8]{1,0:T(8,128)} %adjacency_ref.1, s32[1,8]{1,0:T(1,128)} %bitcast.9, bf16[1024,3072]{1,0:T(8,128)(2,1)} %w_ref.2), custom_call_target="tpu_custom_call" | custom-call | bytes 12582912 | tf_op jit(solution)/shard_map/prepare/pallas_call | solution.py:63
  6.3 0.1 collective-permute-start.3
  6.4 0.1 collective-permute-start.2
  6.5 1.5 %collective-permute-done.refs_1_ = bf16[128,1024]{1,0:T(8,128)(2,1)S(1)} collective-permute-done((bf16[128,1024]{1,0:T(8,128)(2,1)}, bf16[128,1024]{1,0:T(8,128)(2,1)S(1)}, u32[]{:S(2)}, u32[]{:S(2)}) %collective-permute-start) | collective-permute-done | bytes 262176 | tf_op jit(solution)/shard_map/ppermute | solution.py:387
  8.1 3.6 %collective-permute-start.4 = (bf16[128,1024]{1,0:T(8,128)(2,1)S(1)}, bf16[128,1024]{1,0:T(8,128)(2,1)S(1)}, u32[]{:S(2)}, u32[]{:S(2)}) collective-permute-start(bf16[128,1024]{1,0:T(8,128)(2,1)S(1)} %collective-permute-done.refs_1_), channel_id=1, source_target_pairs={{0,1},{1,2},{2,3},{3,4},{4,5},{5,6},{6,7},{7,0},{8,15},{9,8},{10,9... | collective-permute-start | bytes 786440 | tf_op jit(solution)/shard_map/ppermute | solution.py:392
  11.7 1.7 %project.5 = (bf16[1,128,1024]{2,1,0:T(8,128)(2,1)S(1)}, bf16[256,1024]{1,0:T(8,128)(2,1)S(1)}, bf16[1024,256]{1,0:T(8,128)(2,1)S(1)}) custom-call(bf16[128,1024]{1,0:T(8,128)(2,1)S(1)} %copy-done, bf16[128,1024]{1,0:T(8,128)(2,1)S(1)} %collective-permute-done.refs_1_, f32[1,1024]{1,0:T(1,128)S(1)} %bitcast.2, ...), custom_call_target="tpu_custom_call" | custom-call | flops 1073741824 | bytes 5242880 | tf_op jit(solution)/shard_map/project/pallas_call | solution.py:175
  13.4 3.2 %collective-permute-done.3.refs_0_ = bf16[128,1024]{1,0:T(8,128)(2,1)S(1)} collective-permute-done((bf16[128,1024]{1,0:T(8,128)(2,1)S(1)}, bf16[128,1024]{1,0:T(8,128)(2,1)S(1)}, u32[]{:S(2)}, u32[]{:S(2)}) %collective-permute-start.3) | collective-permute-done | bytes 262176 | tf_op jit(solution)/shard_map/ppermute | solution.py:389
  16.6 1.9 %collective-permute-start.1 = (bf16[144,1024]{1,0:T(8,128)(2,1)S(1)}, bf16[144,1024]{1,0:T(8,128)(2,1)S(1)}, u32[]{:S(2)}, u32[]{:S(2)}) collective-permute-start(bf16[144,1024]{1,0:T(8,128)(2,1)S(1)} %get-tuple-element.50.parcel_ref), channel_id=1, source_target_pairs={{8,16},{24,32},{40,48},{56,64},{72,80},{88,96},{104,112},{120,128}... | collective-permute-start | bytes 884744 | tf_op jit(solution)/shard_map/ppermute | solution.py:395
  18.6 0.0 collective-permute-done.2.core_ref
  18.6 0.6 %project_near.1 = (bf16[1,128,1024]{2,1,0:T(8,128)(2,1)S(1)}, f32[8,128]{1,0:T(8,128)S(1)}) custom-call(bf16[144,1024]{1,0:T(8,128)(2,1)S(1)} %collective-permute-done.2.core_ref, bf16[144,1024]{1,0:T(8,128)(2,1)S(1)} %get-tuple-element.50.parcel_ref, f32[1,1024]{1,0:T(1,128)S(1)} %bitcast.3, bf16[1024,1024]{1,0:T(8,128)(2,1)S(1)} %get-tuple-element.51.w_ref.refs_3_), custom_call_target="tpu_custom_call" | custom-call | flops 536870912 | bytes 4194304 | tf_op jit(solution)/shard_map/project_near/pallas_call | solution.py:113
  19.2 0.0 collective-permute-done.4.refs_1_
  19.2 3.3 %collective-permute-start.6 = (bf16[128,1024]{1,0:T(8,128)(2,1)S(1)}, bf16[128,1024]{1,0:T(8,128)(2,1)S(1)}, u32[]{:S(2)}, u32[]{:S(2)}) collective-permute-start(bf16[128,1024]{1,0:T(8,128)(2,1)S(1)} %collective-permute-done.4.refs_1_), channel_id=1, source_target_pairs={{0,1},{1,2},{2,3},{3,4},{4,5},{5,6},{6,7},{7,0},{8,15},{9,8},{10,9... | collective-permute-start | bytes 786440 | tf_op jit(solution)/shard_map/ppermute | solution.py:400
  22.5 1.5 %project.6 = (bf16[256,1024]{1,0:T(8,128)(2,1)S(1)}, bf16[1024,256]{1,0:T(8,128)(2,1)S(1)}) custom-call(bf16[128,1024]{1,0:T(8,128)(2,1)S(1)} %collective-permute-done.3.refs_0_, bf16[128,1024]{1,0:T(8,128)(2,1)S(1)} %collective-permute-done.4.refs_1_, f32[1,1024]{1,0:T(1,128)S(1)} %bitcast.4, bf16[1024,2048]{1,0:T(8,128)(2,1)S(1)} %get-tuple-element.53.refs_4_.refs_3_.refs_2_), custom_call_target="tpu_custom_call" | custom-call | flops 1073741824 | bytes 5242880 | tf_op jit(solution)/shard_map/project/pallas_call | solution.py:175
  24.0 0.2 collective-permute-done.5.refs_0_
  24.2 1.4 %attend.5 = (f32[2,8,256]{2,1,0:T(8,128)S(1)}, f32[2,8,256]{2,1,0:T(8,128)S(1)}, f32[2,1024,128]{2,1,0:T(8,128)S(1)}) custom-call(f32[8,128]{1,0:T(8,128)S(1)} %get-tuple-element.61.refs_0_.info_in, bf16[1,128,1024]{2,1,0:T(8,128)(2,1)S(1)} %get-tuple-element.54.refs_1_, bf16[1,128,1024]{2,1,0:T(8,128)(2,1)S(1)} %get-tuple-element.55.refs_2_, ...), custom_call_target="tpu_custom_call" | custom-call | flops 268435456 | bytes 4194304 | tf_op jit(solution)/shard_map/attend/pallas_call | solution.py:277
  25.7 1.3 %collective-permute-done.6.refs_1_ = bf16[128,1024]{1,0:T(8,128)(2,1)S(1)} collective-permute-done((bf16[128,1024]{1,0:T(8,128)(2,1)S(1)}, bf16[128,1024]{1,0:T(8,128)(2,1)S(1)}, u32[]{:S(2)}, u32[]{:S(2)}) %collective-permute-start.6) | collective-permute-done | bytes 262176 | tf_op jit(solution)/shard_map/ppermute | solution.py:400
  27.0 3.7 %collective-permute-start.8 = (bf16[128,1024]{1,0:T(8,128)(2,1)S(1)}, bf16[128,1024]{1,0:T(8,128)(2,1)S(1)}, u32[]{:S(2)}, u32[]{:S(2)}) collective-permute-start(bf16[128,1024]{1,0:T(8,128)(2,1)S(1)} %collective-permute-done.6.refs_1_), channel_id=1, source_target_pairs={{0,1},{1,2},{2,3},{3,4},{4,5},{5,6},{6,7},{7,0},{8,15},{9,8},{10,9... | collective-permute-start | bytes 786440 | tf_op jit(solution)/shard_map/ppermute | solution.py:408
  30.7 0.6 %project_later.1 = (bf16[1,128,1024]{2,1,0:T(8,128)(2,1)S(1)}, f32[8,128]{1,0:T(8,128)S(1)}) custom-call(bf16[144,1024]{1,0:T(8,128)(2,1)S(1)} %collective-permute-done.1.cross_ref, f32[1,1024]{1,0:T(1,128)S(1)} %bitcast.5, bf16[1024,1024]{1,0:T(8,128)(2,1)S(1)} %get-tuple-element.51.w_ref.refs_3_, f32[8,128]{1,0:T(8,128)S(1)} %get-tuple-element.61.refs_0_.info_in), custom_call_target="tpu_custom_call" | custom-call | flops 268435456 | bytes 3145728 | tf_op jit(solution)/shard_map/project_later/pallas_call | solution.py:135
  31.3 1.5 %attend.6 = (f32[1,8,256]{2,1,0:T(8,128)S(1)}, f32[1,8,256]{2,1,0:T(8,128)S(1)}, f32[1,1024,128]{2,1,0:T(8,128)S(1)}) custom-call(f32[8,128]{1,0:T(8,128)S(1)} %get-tuple-element.62.refs_0_, bf16[1,128,1024]{2,1,0:T(8,128)(2,1)S(1)} %get-tuple-element.75.refs_1_, bf16[256,1024]{1,0:T(8,128)(2,1)S(1)} %get-tuple-element.56.refs_3_.refs_2_, ...), custom_call_target="tpu_custom_call" | custom-call | flops 536870912 | bytes 4194304 | tf_op jit(solution)/shard_map/attend/pallas_call | solution.py:277
  32.8 0.0 collective-permute-done.7.refs_0_
  32.8 0.9 %project.8 = (bf16[128,1024]{1,0:T(8,128)(2,1)S(1)}, bf16[1024,128]{1,0:T(8,128)(2,1)S(1)}) custom-call(bf16[128,1024]{1,0:T(8,128)(2,1)S(1)} %collective-permute-done.7.refs_0_, f32[1,1024]{1,0:T(1,128)S(1)} %bitcast.6, bf16[1024,2048]{1,0:T(8,128)(2,1)S(1)} %get-tuple-element.53.refs_4_.refs_3_.refs_2_), custom_call_target="tpu_custom_call" | custom-call | flops 536870912 | bytes 5242880 | tf_op jit(solution)/shard_map/project/pallas_call | solution.py:175
  33.7 1.5 %project.7 = (bf16[256,1024]{1,0:T(8,128)(2,1)S(1)}, bf16[1024,256]{1,0:T(8,128)(2,1)S(1)}) custom-call(bf16[128,1024]{1,0:T(8,128)(2,1)S(1)} %collective-permute-done.5.refs_0_, bf16[128,1024]{1,0:T(8,128)(2,1)S(1)} %collective-permute-done.6.refs_1_, f32[1,1024]{1,0:T(1,128)S(1)} %bitcast.7, bf16[1024,2048]{1,0:T(8,128)(2,1)S(1)} %get-tuple-element.53.refs_4_.refs_3_.refs_2_), custom_call_target="tpu_custom_call" | custom-call | flops 1073741824 | bytes 5242880 | tf_op jit(solution)/shard_map/project/pallas_call | solution.py:175
  35.1 0.8 %attend.7 = (f32[1,8,256]{2,1,0:T(8,128)S(1)}, f32[1,8,256]{2,1,0:T(8,128)S(1)}, f32[1,1024,128]{2,1,0:T(8,128)S(1)}) custom-call(f32[8,128]{1,0:T(8,128)S(1)} %get-tuple-element.62.refs_0_, bf16[1,128,1024]{2,1,0:T(8,128)(2,1)S(1)} %get-tuple-element.75.refs_1_, ...), custom_call_target="tpu_custom_call", output_to_operand_aliasing={{0}: (6, {}), {1}: (7, {}), {2}: (8, {})} | custom-call | flops 536870912 | bytes 4194304 | tf_op jit(solution)/shard_map/attend/pallas_call | solution.py:277
  35.9 0.9 %project.9 = (bf16[128,1024]{1,0:T(8,128)(2,1)S(1)}, bf16[1024,128]{1,0:T(8,128)(2,1)S(1)}) custom-call(bf16[128,1024]{1,0:T(8,128)(2,1)S(1)} %collective-permute-done.8.refs_0_, f32[1,1024]{1,0:T(1,128)S(1)} %bitcast.8, bf16[1024,2048]{1,0:T(8,128)(2,1)S(1)} %get-tuple-element.53.refs_4_.refs_3_.refs_2_), custom_call_target="tpu_custom_call" | custom-call | flops 536870912 | bytes 5242880 | tf_op jit(solution)/shard_map/project/pallas_call | solution.py:175
  36.8 0.0 copy-start.1
  36.8 0.2 attend.8
  37.0 3.1 %collective-permute-start.9 = (bf16[1088,128]{1,0:T(8,128)(2,1)S(1)}, bf16[1088,128]{1,0:T(8,128)(2,1)S(1)}, u32[]{:S(2)}, u32[]{:S(2)}) collective-permute-start(bf16[1088,128]{1,0:T(8,128)(2,1)S(1)} %get-tuple-element.85), channel_id=1, source_target_pairs={{8,16},{24,32},{40,48},{56,64},{72,80},{88,96},{104,112},{120,128}... | collective-permute-start | bytes 835592 | tf_op jit(solution)/shard_map/ppermute | solution.py:416
  40.1 0.9 %attend.9 = (f32[2,8,256]{2,1,0:T(8,128)S(1)}, f32[2,8,256]{2,1,0:T(8,128)S(1)}, f32[2,1024,128]{2,1,0:T(8,128)S(1)}, bf16[1088,128]{1,0:T(8,128)(2,1)S(1)}) custom-call(f32[8,128]{1,0:T(8,128)S(1)} %get-tuple-element.62.refs_0_, bf16[1,128,1024]{2,1,0:T(8,128)(2,1)S(1)} %get-tuple-element.54.refs_1_, ...), custom_call_target="tpu_custom_call", output_to_operand_aliasing={{0}: (11, {}), {1}: (12, {}), {2}: (13, {})} | custom-call | flops 1073741824 | bytes 4194304 | tf_op jit(solution)/shard_map/attend/pallas_call | solution.py:277
  41.0 0.6 %collective-permute-start.10 = (bf16[1088,128]{1,0:T(8,128)(2,1)S(1)}, bf16[1088,128]{1,0:T(8,128)(2,1)S(1)}, u32[]{:S(2)}, u32[]{:S(2)}) collective-permute-start(bf16[1088,128]{1,0:T(8,128)(2,1)S(1)} %get-tuple-element.92), channel_id=1, source_target_pairs={{0,8},{8,0},{16,24},{24,16},{32,40},{40,32},{48,56},{56,48},{64,72... | collective-permute-start | bytes 835592 | tf_op jit(solution)/shard_map/ppermute | solution.py:420
  41.7 5.4 %collective-permute-done.9.cross_ref = bf16[1088,128]{1,0:T(8,128)(2,1)S(1)} collective-permute-done((bf16[1088,128]{1,0:T(8,128)(2,1)S(1)}, bf16[1088,128]{1,0:T(8,128)(2,1)S(1)}, u32[]{:S(2)}, u32[]{:S(2)}) %collective-permute-start.9) | collective-permute-done | bytes 278560 | tf_op jit(solution)/shard_map/ppermute | solution.py:416
  47.1 1.3 %finish.1 = bf16[128,1024]{1,0:T(8,128)(2,1)} custom-call(f32[2,16,128]{2,1,0:T(8,128)S(1)} %finish_first.1.lse_ref, f32[2,8,256]{2,1,0:T(8,128)S(1)} %get-tuple-element.90.l_ref, f32[2,1024,128]{2,1,0:T(8,128)S(1)} %get-tuple-element.91.own_ref, bf16[1088,128]{1,0:T(8,128)(2,1)S(1)} %collective-permute-done.10.core_ref, ...), custom_call_target="tpu_custom_call" | custom-call | flops 268435456 | bytes 4194304 | tf_op jit(solution)/shard_map/finish/pallas_call | solution.py:351
  (11 shorter events, 0.0 us)
Async XLA Ops:
  0.0 6.3 %copy-start = (bf16[128,1024]{1,0:T(8,128)(2,1)S(1)}, bf16[128,1024]{1,0:T(8,128)(2,1)}, u32[]{:S(2)}) copy-start(bf16[128,1024]{1,0:T(8,128)(2,1)} %features_ref.3) | copy-start | bytes 786436
  0.0 11.7 %copy-start.2 = (f32[1024]{0:T(1024)S(1)}, f32[1024]{0:T(1024)}, u32[]{:S(2)}) copy-start(f32[1024]{0:T(1024)} %param.7) | copy-start | bytes 12292
  0.0 8.1 %collective-permute-start = (bf16[128,1024]{1,0:T(8,128)(2,1)}, bf16[128,1024]{1,0:T(8,128)(2,1)S(1)}, u32[]{:S(2)}, u32[]{:S(2)}) collective-permute-start(bf16[128,1024]{1,0:T(8,128)(2,1)} %features_ref.3), channel_id=1, source_target_pairs={{0,1},{1,2},{2,3},{3,4},{4,5},{5,6},{6,7},{7,0},{8,15},{9,8},{10,9... | collective-permute-start | bytes 786440 | tf_op jit(solution)/shard_map/ppermute | solution.py:387
  6.3 10.3 %collective-permute-start.3 = (bf16[128,1024]{1,0:T(8,128)(2,1)S(1)}, bf16[128,1024]{1,0:T(8,128)(2,1)S(1)}, u32[]{:S(2)}, u32[]{:S(2)}) collective-permute-start(bf16[128,1024]{1,0:T(8,128)(2,1)S(1)} %copy-done), channel_id=1, source_target_pairs={{1,0},{2,1},{3,2},{4,3},{5,4},{6,5},{7,6},{0,7},{15,8},{8,9},{9,10... | collective-permute-start | bytes 786440 | tf_op jit(solution)/shard_map/ppermute | solution.py:389
  6.4 12.1 %collective-permute-start.2 = (bf16[144,1024]{1,0:T(8,128)(2,1)S(1)}, bf16[144,1024]{1,0:T(8,128)(2,1)S(1)}, u32[]{:S(2)}, u32[]{:S(2)}) collective-permute-start(bf16[144,1024]{1,0:T(8,128)(2,1)S(1)} %get-tuple-element.50.parcel_ref), channel_id=1, source_target_pairs={{0,8},{8,0},{16,24},{24,16},{32,40},{40,32},{48,56},{56,48},{64,72... | collective-permute-start | bytes 884744 | tf_op jit(solution)/shard_map/ppermute | solution.py:390
  8.1 11.1 %collective-permute-start.4 = (bf16[128,1024]{1,0:T(8,128)(2,1)S(1)}, bf16[128,1024]{1,0:T(8,128)(2,1)S(1)}, u32[]{:S(2)}, u32[]{:S(2)}) collective-permute-start(bf16[128,1024]{1,0:T(8,128)(2,1)S(1)} %collective-permute-done.refs_1_), channel_id=1, source_target_pairs={{0,1},{1,2},{2,3},{3,4},{4,5},{5,6},{6,7},{7,0},{8,15},{9,8},{10,9... | collective-permute-start | bytes 786440 | tf_op jit(solution)/shard_map/ppermute | solution.py:392
  16.6 7.6 %collective-permute-start.5 = (bf16[128,1024]{1,0:T(8,128)(2,1)S(1)}, bf16[128,1024]{1,0:T(8,128)(2,1)S(1)}, u32[]{:S(2)}, u32[]{:S(2)}) collective-permute-start(bf16[128,1024]{1,0:T(8,128)(2,1)S(1)} %collective-permute-done.3.refs_0_), channel_id=1, source_target_pairs={{1,0},{2,1},{3,2},{4,3},{5,4},{6,5},{7,6},{0,7},{15,8},{8,9},{9,10... | collective-permute-start | bytes 786440 | tf_op jit(solution)/shard_map/ppermute | solution.py:394
  16.6 14.0 %collective-permute-start.1 = (bf16[144,1024]{1,0:T(8,128)(2,1)S(1)}, bf16[144,1024]{1,0:T(8,128)(2,1)S(1)}, u32[]{:S(2)}, u32[]{:S(2)}) collective-permute-start(bf16[144,1024]{1,0:T(8,128)(2,1)S(1)} %get-tuple-element.50.parcel_ref), channel_id=1, source_target_pairs={{8,16},{24,32},{40,48},{56,64},{72,80},{88,96},{104,112},{120,128}... | collective-permute-start | bytes 884744 | tf_op jit(solution)/shard_map/ppermute | solution.py:395
  19.2 7.8 %collective-permute-start.6 = (bf16[128,1024]{1,0:T(8,128)(2,1)S(1)}, bf16[128,1024]{1,0:T(8,128)(2,1)S(1)}, u32[]{:S(2)}, u32[]{:S(2)}) collective-permute-start(bf16[128,1024]{1,0:T(8,128)(2,1)S(1)} %collective-permute-done.4.refs_1_), channel_id=1, source_target_pairs={{0,1},{1,2},{2,3},{3,4},{4,5},{5,6},{6,7},{7,0},{8,15},{9,8},{10,9... | collective-permute-start | bytes 786440 | tf_op jit(solution)/shard_map/ppermute | solution.py:400
  24.2 8.5 %collective-permute-start.7 = (bf16[128,1024]{1,0:T(8,128)(2,1)S(1)}, bf16[128,1024]{1,0:T(8,128)(2,1)S(1)}, u32[]{:S(2)}, u32[]{:S(2)}) collective-permute-start(bf16[128,1024]{1,0:T(8,128)(2,1)S(1)} %collective-permute-done.5.refs_0_), channel_id=1, source_target_pairs={{1,0},{2,1},{3,2},{4,3},{5,4},{6,5},{7,6},{0,7},{15,8},{8,9},{9,10... | collective-permute-start | bytes 786440 | tf_op jit(solution)/shard_map/ppermute | solution.py:402
  27.0 9.0 %collective-permute-start.8 = (bf16[128,1024]{1,0:T(8,128)(2,1)S(1)}, bf16[128,1024]{1,0:T(8,128)(2,1)S(1)}, u32[]{:S(2)}, u32[]{:S(2)}) collective-permute-start(bf16[128,1024]{1,0:T(8,128)(2,1)S(1)} %collective-permute-done.6.refs_1_), channel_id=1, source_target_pairs={{0,1},{1,2},{2,3},{3,4},{4,5},{5,6},{6,7},{7,0},{8,15},{9,8},{10,9... | collective-permute-start | bytes 786440 | tf_op jit(solution)/shard_map/ppermute | solution.py:408
  36.8 10.3 %copy-start.1 = (bf16[1024,1024]{1,0:T(8,128)(2,1)S(1)}, bf16[1024,1024]{1,0:T(8,128)(2,1)}, u32[]{:S(2)}) copy-start(bf16[1024,1024]{1,0:T(8,128)(2,1)} %w_ref.3) | copy-start | bytes 6291460
  37.0 10.1 %collective-permute-start.9 = (bf16[1088,128]{1,0:T(8,128)(2,1)S(1)}, bf16[1088,128]{1,0:T(8,128)(2,1)S(1)}, u32[]{:S(2)}, u32[]{:S(2)}) collective-permute-start(bf16[1088,128]{1,0:T(8,128)(2,1)S(1)} %get-tuple-element.85), channel_id=1, source_target_pairs={{8,16},{24,32},{40,48},{56,64},{72,80},{88,96},{104,112},{120,128}... | collective-permute-start | bytes 835592 | tf_op jit(solution)/shard_map/ppermute | solution.py:416
  41.0 6.1 %collective-permute-start.10 = (bf16[1088,128]{1,0:T(8,128)(2,1)S(1)}, bf16[1088,128]{1,0:T(8,128)(2,1)S(1)}, u32[]{:S(2)}, u32[]{:S(2)}) collective-permute-start(bf16[1088,128]{1,0:T(8,128)(2,1)S(1)} %get-tuple-element.92), channel_id=1, source_target_pairs={{0,8},{8,0},{16,24},{24,16},{32,40},{40,32},{48,56},{56,48},{64,72... | collective-permute-start | bytes 835592 | tf_op jit(solution)/shard_map/ppermute | solution.py:420

commit v4 on v3

--- a/solution.py
+++ b/solution.py
@@ -397,7 +397,7 @@
     kv_a = ((0, -1), *kv_a)
     pair = [(q_own, 0, 0), (q_core, 1, 0)]
 
-    one.append(lax.ppermute(tied(one[1], q_core), *up))
+    one.append(lax.ppermute(tied(one[1], kv_a[1]), *up))
     kv_b = project([two[0], one[1]], gain, w_kv)
     two.append(lax.ppermute(tied(two[1], *kv_b), *down))
     kv_b = ((1, -2), *kv_b)

time: 49.2 us -> 52.4 us (1.065)
  waiting for transfers between devices: 11.8 us -> 13.4 us
  starting transfers between devices: 19.5 us -> 20.8 us
  Pallas kernels: 16.9 us -> 17.6 us
    ppermute x1, starting transfers between devices: 1.91 us -> 4.95 us  [body(): from_row = lax.ppermute(tied(parcel, one[0]), 'dom', hop)]
    ppermute x1, waiting for transfers between devices: 1.29 us -> 2.84 us  [body(): one.append(lax.ppermute(tied(one[1], kv_a[1]), *up))]
    ppermute x1, starting transfers between devices: 3.09 us -> 1.92 us  [body(): cross = lax.ppermute(to_cross, 'dom', hop)]
    ppermute x1, waiting for transfers between devices: 0.01 us -> 1.1 us  [body(): two.append(lax.ppermute(tied(two[1], *kv_b), *down))]
    pallas_call x5, Pallas kernels: 4.78 us -> 5.46 us  [attend(): pl.pallas_call(functools.partial(attend_kernel, who, steps, not state, la...]
    ppermute x1, starting transfers between devices: 0.65 us -> 0.09 us  [body(): core = lax.ppermute(to_core, 'dom', swap)]
  transfers between devices with their start and end apart: 11 -> 11, of which waited for: 5 -> 5; matrix products, arithmetic and copies ran while one was open for 0% -> 0% of each run, Pallas kernels for 30% -> 28%
where the time goes in v4:
time: 52.4 us; the launch traced here: 52.2 us
  starting transfers between devices  20.8 us (40%)
  Pallas kernels  17.6 us (34%)
  waiting for transfers between devices  13.4 us (26%)
    pallas_call x5, Pallas kernels, project(): pl.pallas_call(functools.partial(project_kernel, len(arrays), query), in_...  6.4 us
    pallas_call x5, Pallas kernels, attend(): pl.pallas_call(functools.partial(attend_kernel, who, steps, not state, la...  5.46 us
    ppermute x1, waiting for transfers between devices, body(): cross = lax.ppermute(to_cross, 'dom', hop)  5.07 us
    ppermute x1, starting transfers between devices, body(): from_row = lax.ppermute(tied(parcel, one[0]), 'dom', hop)  4.95 us
    ppermute x1, starting transfers between devices, body(): one.append(lax.ppermute(tied(one[2], kv_b[1]), *up))  3.69 us
    ppermute x1, starting transfers between devices, body(): one.append(lax.ppermute(tied(one[0], w_query), *up))  3.59 us
    ppermute x1, starting transfers between devices, body(): one.append(lax.ppermute(tied(one[1], kv_a[1]), *up))  3.31 us
    pallas_call x1, Pallas kernels, prepare(): pl.pallas_call(prepare_kernel, in_specs=[pl.BlockSpec(memory_space=pltpu....  3.2 us
  transfers between devices with their start and end apart: 11, of which 5 were waited for; matrix products, arithmetic and copies ran while one was open for 0% of the time, Pallas kernels for 28%

profile of v4, /device:TPU:120, one launch (start us, length us, event | category | flops | bytes accessed | tf_op | source)
XLA Modules:
  0.0 52.2 jit_solution(8916366455274613702)
XLA Ops:
  0.0 3.1 %collective-permute-start = (bf16[128,1024]{1,0:T(8,128)(2,1)}, bf16[128,1024]{1,0:T(8,128)(2,1)S(1)}, u32[]{:S(2)}, u32[]{:S(2)}) collective-permute-start(bf16[128,1024]{1,0:T(8,128)(2,1)} %features_ref.3), channel_id=1, source_target_pairs={{0,1},{1,2},{2,3},{3,4},{4,5},{5,6},{6,7},{7,0},{8,15},{9,8},{10,9... | collective-permute-start | bytes 786440 | tf_op jit(solution)/shard_map/ppermute | solution.py:387
  3.1 3.2 %prepare.1 = (bf16[144,1024]{1,0:T(8,128)(2,1)S(1)}, bf16[1024,1024]{1,0:T(8,128)(2,1)S(1)}, bf16[1024,2048]{1,0:T(8,128)(2,1)S(1)}) custom-call(bf16[128,1024]{1,0:T(8,128)(2,1)} %features_ref.3, s32[8,8]{1,0:T(8,128)} %adjacency_ref.1, s32[1,8]{1,0:T(1,128)} %bitcast.9, bf16[1024,3072]{1,0:T(8,128)(2,1)} %w_ref.2), custom_call_target="tpu_custom_call" | custom-call | bytes 12582912 | tf_op jit(solution)/shard_map/prepare/pallas_call | solution.py:63
  6.3 0.1 collective-permute-start.3
  6.4 1.6 %collective-permute-done.refs_1_ = bf16[128,1024]{1,0:T(8,128)(2,1)S(1)} collective-permute-done((bf16[128,1024]{1,0:T(8,128)(2,1)}, bf16[128,1024]{1,0:T(8,128)(2,1)S(1)}, u32[]{:S(2)}, u32[]{:S(2)}) %collective-permute-start) | collective-permute-done | bytes 262176 | tf_op jit(solution)/shard_map/ppermute | solution.py:387
  8.1 3.6 %collective-permute-start.4 = (bf16[128,1024]{1,0:T(8,128)(2,1)S(1)}, bf16[128,1024]{1,0:T(8,128)(2,1)S(1)}, u32[]{:S(2)}, u32[]{:S(2)}) collective-permute-start(bf16[128,1024]{1,0:T(8,128)(2,1)S(1)} %collective-permute-done.refs_1_), channel_id=1, source_target_pairs={{0,1},{1,2},{2,3},{3,4},{4,5},{5,6},{6,7},{7,0},{8,15},{9,8},{10,9... | collective-permute-start | bytes 786440 | tf_op jit(solution)/shard_map/ppermute | solution.py:392
  11.7 1.7 %project.5 = (bf16[1,128,1024]{2,1,0:T(8,128)(2,1)S(1)}, bf16[256,1024]{1,0:T(8,128)(2,1)S(1)}, bf16[1024,256]{1,0:T(8,128)(2,1)S(1)}) custom-call(bf16[128,1024]{1,0:T(8,128)(2,1)S(1)} %copy-done, bf16[128,1024]{1,0:T(8,128)(2,1)S(1)} %collective-permute-done.refs_1_, f32[1,1024]{1,0:T(1,128)S(1)} %bitcast.2, ...), custom_call_target="tpu_custom_call" | custom-call | flops 1073741824 | bytes 5242880 | tf_op jit(solution)/shard_map/project/pallas_call | solution.py:175
  13.4 2.7 %collective-permute-done.3.refs_0_ = bf16[128,1024]{1,0:T(8,128)(2,1)S(1)} collective-permute-done((bf16[128,1024]{1,0:T(8,128)(2,1)S(1)}, bf16[128,1024]{1,0:T(8,128)(2,1)S(1)}, u32[]{:S(2)}, u32[]{:S(2)}) %collective-permute-start.3) | collective-permute-done | bytes 262176 | tf_op jit(solution)/shard_map/ppermute | solution.py:389
  16.1 0.0 collective-permute-start.5
  16.2 0.0 collective-permute-start.2
  16.2 4.9 %collective-permute-start.1 = (bf16[144,1024]{1,0:T(8,128)(2,1)S(1)}, bf16[144,1024]{1,0:T(8,128)(2,1)S(1)}, u32[]{:S(2)}, u32[]{:S(2)}) collective-permute-start(bf16[144,1024]{1,0:T(8,128)(2,1)S(1)} %get-tuple-element.50.parcel_ref), channel_id=1, source_target_pairs={{8,16},{24,32},{40,48},{56,64},{72,80},{88,96},{104,112},{120,128}... | collective-permute-start | bytes 884744 | tf_op jit(solution)/shard_map/ppermute | solution.py:395
  21.1 0.0 collective-permute-done.4.refs_1_
  21.1 3.3 %collective-permute-start.6 = (bf16[128,1024]{1,0:T(8,128)(2,1)S(1)}, bf16[128,1024]{1,0:T(8,128)(2,1)S(1)}, u32[]{:S(2)}, u32[]{:S(2)}) collective-permute-start(bf16[128,1024]{1,0:T(8,128)(2,1)S(1)} %collective-permute-done.4.refs_1_), channel_id=1, source_target_pairs={{0,1},{1,2},{2,3},{3,4},{4,5},{5,6},{6,7},{7,0},{8,15},{9,8},{10,9... | collective-permute-start | bytes 786440 | tf_op jit(solution)/shard_map/ppermute | solution.py:400
  24.4 1.5 %project.6 = (bf16[256,1024]{1,0:T(8,128)(2,1)S(1)}, bf16[1024,256]{1,0:T(8,128)(2,1)S(1)}) custom-call(bf16[128,1024]{1,0:T(8,128)(2,1)S(1)} %collective-permute-done.3.refs_0_, bf16[128,1024]{1,0:T(8,128)(2,1)S(1)} %collective-permute-done.4.refs_1_, f32[1,1024]{1,0:T(1,128)S(1)} %bitcast.3, bf16[1024,2048]{1,0:T(8,128)(2,1)S(1)} %get-tuple-element.53.refs_4_.refs_3_.refs_2_), custom_call_target="tpu_custom_call" | custom-call | flops 1073741824 | bytes 5242880 | tf_op jit(solution)/shard_map/project/pallas_call | solution.py:175
  25.9 0.1 collective-permute-start.7
  26.0 0.6 %project_near.1 = (bf16[1,128,1024]{2,1,0:T(8,128)(2,1)S(1)}, f32[8,128]{1,0:T(8,128)S(1)}) custom-call(bf16[144,1024]{1,0:T(8,128)(2,1)S(1)} %collective-permute-done.2.core_ref, bf16[144,1024]{1,0:T(8,128)(2,1)S(1)} %get-tuple-element.50.parcel_ref, f32[1,1024]{1,0:T(1,128)S(1)} %bitcast.4, bf16[1024,1024]{1,0:T(8,128)(2,1)S(1)} %get-tuple-element.51.w_ref.refs_3_), custom_call_target="tpu_custom_call" | custom-call | flops 536870912 | bytes 4194304 | tf_op jit(solution)/shard_map/project_near/pallas_call | solution.py:113
  26.6 0.8 %attend.5 = (f32[2,8,256]{2,1,0:T(8,128)S(1)}, f32[2,8,256]{2,1,0:T(8,128)S(1)}, f32[2,1024,128]{2,1,0:T(8,128)S(1)}) custom-call(f32[8,128]{1,0:T(8,128)S(1)} %get-tuple-element.61.refs_0_.info_in, bf16[1,128,1024]{2,1,0:T(8,128)(2,1)S(1)} %get-tuple-element.54.refs_1_, bf16[1,128,1024]{2,1,0:T(8,128)(2,1)S(1)} %get-tuple-element.55.refs_2_, ...), custom_call_target="tpu_custom_call" | custom-call | flops 268435456 | bytes 4194304 | tf_op jit(solution)/shard_map/attend/pallas_call | solution.py:277
  27.4 2.8 %collective-permute-done.6.refs_1_ = bf16[128,1024]{1,0:T(8,128)(2,1)S(1)} collective-permute-done((bf16[128,1024]{1,0:T(8,128)(2,1)S(1)}, bf16[128,1024]{1,0:T(8,128)(2,1)S(1)}, u32[]{:S(2)}, u32[]{:S(2)}) %collective-permute-start.6) | collective-permute-done | bytes 262176 | tf_op jit(solution)/shard_map/ppermute | solution.py:400
  30.3 3.7 %collective-permute-start.8 = (bf16[128,1024]{1,0:T(8,128)(2,1)S(1)}, bf16[128,1024]{1,0:T(8,128)(2,1)S(1)}, u32[]{:S(2)}, u32[]{:S(2)}) collective-permute-start(bf16[128,1024]{1,0:T(8,128)(2,1)S(1)} %collective-permute-done.6.refs_1_), channel_id=1, source_target_pairs={{0,1},{1,2},{2,3},{3,4},{4,5},{5,6},{6,7},{7,0},{8,15},{9,8},{10,9... | collective-permute-start | bytes 786440 | tf_op jit(solution)/shard_map/ppermute | solution.py:408
  34.0 0.6 %project_later.1 = (bf16[1,128,1024]{2,1,0:T(8,128)(2,1)S(1)}, f32[8,128]{1,0:T(8,128)S(1)}) custom-call(bf16[144,1024]{1,0:T(8,128)(2,1)S(1)} %collective-permute-done.1.cross_ref, f32[1,1024]{1,0:T(1,128)S(1)} %bitcast.5, bf16[1024,1024]{1,0:T(8,128)(2,1)S(1)} %get-tuple-element.51.w_ref.refs_3_, f32[8,128]{1,0:T(8,128)S(1)} %get-tuple-element.61.refs_0_.info_in), custom_call_target="tpu_custom_call" | custom-call | flops 268435456 | bytes 3145728 | tf_op jit(solution)/shard_map/project_later/pallas_call | solution.py:135
  34.6 0.2 attend.6
  34.8 1.1 %collective-permute-done.7.refs_0_ = bf16[128,1024]{1,0:T(8,128)(2,1)S(1)} collective-permute-done((bf16[128,1024]{1,0:T(8,128)(2,1)S(1)}, bf16[128,1024]{1,0:T(8,128)(2,1)S(1)}, u32[]{:S(2)}, u32[]{:S(2)}) %collective-permute-start.7) | collective-permute-done | bytes 262176 | tf_op jit(solution)/shard_map/ppermute | solution.py:402
  35.9 0.9 %project.8 = (bf16[128,1024]{1,0:T(8,128)(2,1)S(1)}, bf16[1024,128]{1,0:T(8,128)(2,1)S(1)}) custom-call(bf16[128,1024]{1,0:T(8,128)(2,1)S(1)} %collective-permute-done.7.refs_0_, f32[1,1024]{1,0:T(1,128)S(1)} %bitcast.6, bf16[1024,2048]{1,0:T(8,128)(2,1)S(1)} %get-tuple-element.53.refs_4_.refs_3_.refs_2_), custom_call_target="tpu_custom_call" | custom-call | flops 536870912 | bytes 5242880 | tf_op jit(solution)/shard_map/project/pallas_call | solution.py:175
  36.8 1.5 %project.7 = (bf16[256,1024]{1,0:T(8,128)(2,1)S(1)}, bf16[1024,256]{1,0:T(8,128)(2,1)S(1)}) custom-call(bf16[128,1024]{1,0:T(8,128)(2,1)S(1)} %collective-permute-done.5.refs_0_, bf16[128,1024]{1,0:T(8,128)(2,1)S(1)} %collective-permute-done.6.refs_1_, f32[1,1024]{1,0:T(1,128)S(1)} %bitcast.7, bf16[1024,2048]{1,0:T(8,128)(2,1)S(1)} %get-tuple-element.53.refs_4_.refs_3_.refs_2_), custom_call_target="tpu_custom_call" | custom-call | flops 1073741824 | bytes 5242880 | tf_op jit(solution)/shard_map/project/pallas_call | solution.py:175
  38.2 0.8 %attend.7 = (f32[1,8,256]{2,1,0:T(8,128)S(1)}, f32[1,8,256]{2,1,0:T(8,128)S(1)}, f32[1,1024,128]{2,1,0:T(8,128)S(1)}) custom-call(f32[8,128]{1,0:T(8,128)S(1)} %get-tuple-element.62.refs_0_, bf16[1,128,1024]{2,1,0:T(8,128)(2,1)S(1)} %get-tuple-element.75.refs_1_, ...), custom_call_target="tpu_custom_call", output_to_operand_aliasing={{0}: (6, {}), {1}: (7, {}), {2}: (8, {})} | custom-call | flops 536870912 | bytes 4194304 | tf_op jit(solution)/shard_map/attend/pallas_call | solution.py:277
  39.1 0.9 %project.9 = (bf16[128,1024]{1,0:T(8,128)(2,1)S(1)}, bf16[1024,128]{1,0:T(8,128)(2,1)S(1)}) custom-call(bf16[128,1024]{1,0:T(8,128)(2,1)S(1)} %collective-permute-done.8.refs_0_, f32[1,1024]{1,0:T(1,128)S(1)} %bitcast.8, bf16[1024,2048]{1,0:T(8,128)(2,1)S(1)} %get-tuple-element.53.refs_4_.refs_3_.refs_2_), custom_call_target="tpu_custom_call" | custom-call | flops 536870912 | bytes 5242880 | tf_op jit(solution)/shard_map/project/pallas_call | solution.py:175
  39.9 0.0 copy-start.1
  39.9 0.8 %attend.8 = (f32[1,8,256]{2,1,0:T(8,128)S(1)}, f32[1,8,256]{2,1,0:T(8,128)S(1)}, f32[1,1024,128]{2,1,0:T(8,128)S(1)}, bf16[1088,128]{1,0:T(8,128)(2,1)S(1)}) custom-call(f32[8,128]{1,0:T(8,128)S(1)} %get-tuple-element.62.refs_0_, bf16[1,128,1024]{2,1,0:T(8,128)(2,1)S(1)} %get-tuple-element.75.refs_1_, ...), custom_call_target="tpu_custom_call", output_to_operand_aliasing={{0}: (4, {}), {1}: (5, {}), {2}: (6, {})} | custom-call | flops 268435456 | bytes 4194304 | tf_op jit(solution)/shard_map/attend/pallas_call | solution.py:277
  40.8 1.9 %collective-permute-start.9 = (bf16[1088,128]{1,0:T(8,128)(2,1)S(1)}, bf16[1088,128]{1,0:T(8,128)(2,1)S(1)}, u32[]{:S(2)}, u32[]{:S(2)}) collective-permute-start(bf16[1088,128]{1,0:T(8,128)(2,1)S(1)} %get-tuple-element.85), channel_id=1, source_target_pairs={{8,16},{24,32},{40,48},{56,64},{72,80},{88,96},{104,112},{120,128}... | collective-permute-start | bytes 835592 | tf_op jit(solution)/shard_map/ppermute | solution.py:416
  42.7 2.9 %attend.9 = (f32[2,8,256]{2,1,0:T(8,128)S(1)}, f32[2,8,256]{2,1,0:T(8,128)S(1)}, f32[2,1024,128]{2,1,0:T(8,128)S(1)}, bf16[1088,128]{1,0:T(8,128)(2,1)S(1)}) custom-call(f32[8,128]{1,0:T(8,128)S(1)} %get-tuple-element.62.refs_0_, bf16[1,128,1024]{2,1,0:T(8,128)(2,1)S(1)} %get-tuple-element.54.refs_1_, ...), custom_call_target="tpu_custom_call", output_to_operand_aliasing={{0}: (11, {}), {1}: (12, {}), {2}: (13, {})} | custom-call | flops 1073741824 | bytes 4194304 | tf_op jit(solution)/shard_map/attend/pallas_call | solution.py:277
  45.6 0.1 collective-permute-start.10
  45.7 5.1 %collective-permute-done.9.cross_ref = bf16[1088,128]{1,0:T(8,128)(2,1)S(1)} collective-permute-done((bf16[1088,128]{1,0:T(8,128)(2,1)S(1)}, bf16[1088,128]{1,0:T(8,128)(2,1)S(1)}, u32[]{:S(2)}, u32[]{:S(2)}) %collective-permute-start.9) | collective-permute-done | bytes 278560 | tf_op jit(solution)/shard_map/ppermute | solution.py:416
  50.8 1.3 %finish.1 = bf16[128,1024]{1,0:T(8,128)(2,1)} custom-call(f32[2,16,128]{2,1,0:T(8,128)S(1)} %finish_first.1.lse_ref, f32[2,8,256]{2,1,0:T(8,128)S(1)} %get-tuple-element.90.l_ref, f32[2,1024,128]{2,1,0:T(8,128)S(1)} %get-tuple-element.91.own_ref, bf16[1088,128]{1,0:T(8,128)(2,1)S(1)} %collective-permute-done.10.core_ref, ...), custom_call_target="tpu_custom_call" | custom-call | flops 268435456 | bytes 4194304 | tf_op jit(solution)/shard_map/finish/pallas_call | solution.py:351
  (11 shorter events, 0.0 us)
Async XLA Ops:
  0.0 6.3 %copy-start = (bf16[128,1024]{1,0:T(8,128)(2,1)S(1)}, bf16[128,1024]{1,0:T(8,128)(2,1)}, u32[]{:S(2)}) copy-start(bf16[128,1024]{1,0:T(8,128)(2,1)} %features_ref.3) | copy-start | bytes 786436
  0.0 11.7 %copy-start.2 = (f32[1024]{0:T(1024)S(1)}, f32[1024]{0:T(1024)}, u32[]{:S(2)}) copy-start(f32[1024]{0:T(1024)} %param.7) | copy-start | bytes 12292
  0.0 8.1 %collective-permute-start = (bf16[128,1024]{1,0:T(8,128)(2,1)}, bf16[128,1024]{1,0:T(8,128)(2,1)S(1)}, u32[]{:S(2)}, u32[]{:S(2)}) collective-permute-start(bf16[128,1024]{1,0:T(8,128)(2,1)} %features_ref.3), channel_id=1, source_target_pairs={{0,1},{1,2},{2,3},{3,4},{4,5},{5,6},{6,7},{7,0},{8,15},{9,8},{10,9... | collective-permute-start | bytes 786440 | tf_op jit(solution)/shard_map/ppermute | solution.py:387
  6.3 9.8 %collective-permute-start.3 = (bf16[128,1024]{1,0:T(8,128)(2,1)S(1)}, bf16[128,1024]{1,0:T(8,128)(2,1)S(1)}, u32[]{:S(2)}, u32[]{:S(2)}) collective-permute-start(bf16[128,1024]{1,0:T(8,128)(2,1)S(1)} %copy-done), channel_id=1, source_target_pairs={{1,0},{2,1},{3,2},{4,3},{5,4},{6,5},{7,6},{0,7},{15,8},{8,9},{9,10... | collective-permute-start | bytes 786440 | tf_op jit(solution)/shard_map/ppermute | solution.py:389
  8.1 13.0 %collective-permute-start.4 = (bf16[128,1024]{1,0:T(8,128)(2,1)S(1)}, bf16[128,1024]{1,0:T(8,128)(2,1)S(1)}, u32[]{:S(2)}, u32[]{:S(2)}) collective-permute-start(bf16[128,1024]{1,0:T(8,128)(2,1)S(1)} %collective-permute-done.refs_1_), channel_id=1, source_target_pairs={{0,1},{1,2},{2,3},{3,4},{4,5},{5,6},{6,7},{7,0},{8,15},{9,8},{10,9... | collective-permute-start | bytes 786440 | tf_op jit(solution)/shard_map/ppermute | solution.py:392
  16.1 9.8 %collective-permute-start.5 = (bf16[128,1024]{1,0:T(8,128)(2,1)S(1)}, bf16[128,1024]{1,0:T(8,128)(2,1)S(1)}, u32[]{:S(2)}, u32[]{:S(2)}) collective-permute-start(bf16[128,1024]{1,0:T(8,128)(2,1)S(1)} %collective-permute-done.3.refs_0_), channel_id=1, source_target_pairs={{1,0},{2,1},{3,2},{4,3},{5,4},{6,5},{7,6},{0,7},{15,8},{8,9},{9,10... | collective-permute-start | bytes 786440 | tf_op jit(solution)/shard_map/ppermute | solution.py:394
  16.2 9.9 %collective-permute-start.2 = (bf16[144,1024]{1,0:T(8,128)(2,1)S(1)}, bf16[144,1024]{1,0:T(8,128)(2,1)S(1)}, u32[]{:S(2)}, u32[]{:S(2)}) collective-permute-start(bf16[144,1024]{1,0:T(8,128)(2,1)S(1)} %get-tuple-element.50.parcel_ref), channel_id=1, source_target_pairs={{0,8},{8,0},{16,24},{24,16},{32,40},{40,32},{48,56},{56,48},{64,72... | collective-permute-start | bytes 884744 | tf_op jit(solution)/shard_map/ppermute | solution.py:390
  16.2 17.8 %collective-permute-start.1 = (bf16[144,1024]{1,0:T(8,128)(2,1)S(1)}, bf16[144,1024]{1,0:T(8,128)(2,1)S(1)}, u32[]{:S(2)}, u32[]{:S(2)}) collective-permute-start(bf16[144,1024]{1,0:T(8,128)(2,1)S(1)} %get-tuple-element.50.parcel_ref), channel_id=1, source_target_pairs={{8,16},{24,32},{40,48},{56,64},{72,80},{88,96},{104,112},{120,128}... | collective-permute-start | bytes 884744 | tf_op jit(solution)/shard_map/ppermute | solution.py:395
  21.1 9.2 %collective-permute-start.6 = (bf16[128,1024]{1,0:T(8,128)(2,1)S(1)}, bf16[128,1024]{1,0:T(8,128)(2,1)S(1)}, u32[]{:S(2)}, u32[]{:S(2)}) collective-permute-start(bf16[128,1024]{1,0:T(8,128)(2,1)S(1)} %collective-permute-done.4.refs_1_), channel_id=1, source_target_pairs={{0,1},{1,2},{2,3},{3,4},{4,5},{5,6},{6,7},{7,0},{8,15},{9,8},{10,9... | collective-permute-start | bytes 786440 | tf_op jit(solution)/shard_map/ppermute | solution.py:400
  25.9 10.0 %collective-permute-start.7 = (bf16[128,1024]{1,0:T(8,128)(2,1)S(1)}, bf16[128,1024]{1,0:T(8,128)(2,1)S(1)}, u32[]{:S(2)}, u32[]{:S(2)}) collective-permute-start(bf16[128,1024]{1,0:T(8,128)(2,1)S(1)} %collective-permute-done.5.refs_0_), channel_id=1, source_target_pairs={{1,0},{2,1},{3,2},{4,3},{5,4},{6,5},{7,6},{0,7},{15,8},{8,9},{9,10... | collective-permute-start | bytes 786440 | tf_op jit(solution)/shard_map/ppermute | solution.py:402
  30.3 8.8 %collective-permute-start.8 = (bf16[128,1024]{1,0:T(8,128)(2,1)S(1)}, bf16[128,1024]{1,0:T(8,128)(2,1)S(1)}, u32[]{:S(2)}, u32[]{:S(2)}) collective-permute-start(bf16[128,1024]{1,0:T(8,128)(2,1)S(1)} %collective-permute-done.6.refs_1_), channel_id=1, source_target_pairs={{0,1},{1,2},{2,3},{3,4},{4,5},{5,6},{6,7},{7,0},{8,15},{9,8},{10,9... | collective-permute-start | bytes 786440 | tf_op jit(solution)/shard_map/ppermute | solution.py:408
  39.9 10.9 %copy-start.1 = (bf16[1024,1024]{1,0:T(8,128)(2,1)S(1)}, bf16[1024,1024]{1,0:T(8,128)(2,1)}, u32[]{:S(2)}) copy-start(bf16[1024,1024]{1,0:T(8,128)(2,1)} %w_ref.3) | copy-start | bytes 6291460
  40.8 10.0 %collective-permute-start.9 = (bf16[1088,128]{1,0:T(8,128)(2,1)S(1)}, bf16[1088,128]{1,0:T(8,128)(2,1)S(1)}, u32[]{:S(2)}, u32[]{:S(2)}) collective-permute-start(bf16[1088,128]{1,0:T(8,128)(2,1)S(1)} %get-tuple-element.85), channel_id=1, source_target_pairs={{8,16},{24,32},{40,48},{56,64},{72,80},{88,96},{104,112},{120,128}... | collective-permute-start | bytes 835592 | tf_op jit(solution)/shard_map/ppermute | solution.py:416
  45.6 5.2 %collective-permute-start.10 = (bf16[1088,128]{1,0:T(8,128)(2,1)S(1)}, bf16[1088,128]{1,0:T(8,128)(2,1)S(1)}, u32[]{:S(2)}, u32[]{:S(2)}) collective-permute-start(bf16[1088,128]{1,0:T(8,128)(2,1)S(1)} %get-tuple-element.92), channel_id=1, source_target_pairs={{0,8},{8,0},{16,24},{24,16},{32,40},{40,32},{48,56},{56,48},{64,72... | collective-permute-start | bytes 835592 | tf_op jit(solution)/shard_map/ppermute | solution.py:420
